TPU v7x, 32 devices: a whole 2x2x4 slice. The times are simulated.
32 devices in a mesh: dp: 8 (over y, x, core), seq: 4 (over z).
Axes of the slice: x: 2, y: 2, z: 4, core: 2. Of those that a mesh axis runs over, the one named last changes fastest.
Arguments:
- tokens: bfloat16 [32, 1024, 576], P('dp', 'seq'), may hold values from -6 to 6
- lengths: int32 [32], P('dp'), may hold values from 256 to 1024, as said below
- w_query: bfloat16 [576, 576], replicated, may hold values from -0.25 to 0.25
- w_key: bfloat16 [576, 192], replicated, may hold values from -0.25 to 0.25
- w_value: bfloat16 [576, 192], replicated, may hold values from -0.25 to 0.25
- w_out: bfloat16 [576, 576], replicated, may hold values from -1 to 1
- w_gate: bfloat16 [576, 1536], replicated, may hold values from -0.25 to 0.25
- w_up: bfloat16 [576, 1536], replicated, may hold values from -0.25 to 0.25
- w_down: bfloat16 [1536, 576], replicated, may hold values from -0.15625 to 0.15625
- gain_attn: float32 [576], replicated, may hold values from 0.1 to 1.9
- gain_ffn: float32 [576], replicated, may hold values from 0.1 to 1.9
- cotangent: bfloat16 [32, 1024, 576], P('dp', 'seq'), may hold values from -6 to 6
Outputs:
- mixed: bfloat16 [32, 1024, 576], P('dp', 'seq')
- tokens_grad: bfloat16 [32, 1024, 576], P('dp', 'seq')
- w_query_grad: float32 [576, 576], replicated
- w_key_grad: float32 [576, 192], replicated
- w_value_grad: float32 [576, 192], replicated
- w_out_grad: float32 [576, 576], replicated
- w_gate_grad: float32 [576, 1536], replicated
- w_up_grad: float32 [576, 1536], replicated
- w_down_grad: float32 [1536, 576], replicated
- gain_attn_grad: float32 [576], replicated
- gain_ffn_grad: float32 [576], replicated
Inputs may be any that keep to these rules, and one draw needn't show every extreme that they name: A row's real tokens are its first lengths entries; among the 4 rows of each index of dp one row has exactly 1024.
All inputs are finite; a program needn't handle non-finite values.
Results may differ from a plain program's by a relative error of at most 0.03.
Values may be sent and summed in bfloat16 or wider, within the bound.
No kernel may reach another device: no remote copies, remote signals or barrier semaphores. Data moves between devices by JAX's collectives and lax.ppermute only.
A program may use at most 128 MiB of HBM per device.

v0:
```python
from functools import partial
import math

import jax
import jax.numpy as jnp
from jax import lax
from jax.experimental import pallas as pl
from jax.experimental.pallas import tpu as pltpu
from jax.sharding import PartitionSpec as P

HQ = 9
HK = 3
DH = 64


eps_norm = 1e-05
rope_base = 100000.0
neg_large = -1e30


def norm_rows(values, gain_vec):
    return (
        values * lax.rsqrt(jnp.mean(values * values, axis=-1, keepdims=True) + eps_norm) * gain_vec
    )


def rotate(values, positions, turn_sign):
    half_dim = values.shape[-1] // 2
    frequency = rope_base ** (-jnp.arange(half_dim, dtype=jnp.float32) / half_dim)
    angles = turn_sign * positions.astype(jnp.float32)[:, None] * frequency[None, :]
    cosine = jnp.cos(angles)[:, None, :]
    sine_part = jnp.sin(angles)[:, None, :]
    first_half = values[..., :half_dim]
    second_half = values[..., half_dim:]
    return jnp.concatenate(
        [
            first_half * cosine - second_half * sine_part,
            second_half * cosine + first_half * sine_part,
        ],
        axis=-1,
    )


def inner_rows(left, right):
    return lax.dot_general(
        left, right, (((0,), (0,)), ((), ())), preferred_element_type=jnp.float32
    )


def times_t(left, right):
    return lax.dot_general(
        left, right, (((1,), (1,)), ((), ())), preferred_element_type=jnp.float32
    )


def fold_piece(block_len, step_fn, carry, pieces):
    piece_count = pieces.shape[1] // block_len

    def inner_step(index_step, state):
        part_piece = lax.dynamic_slice_in_dim(pieces, index_step * block_len, block_len, 1)
        return step_fn(state, part_piece, index_step * block_len)

    return lax.fori_loop(0, piece_count, inner_step, carry)


def local_general(
    tokens,
    lengths,
    w_query,
    w_key,
    w_value,
    w_out,
    w_gate,
    w_up,
    w_down,
    gain_attn,
    gain_ffn,
    cotangent,
):
    row_count, block_len, model_width = tokens.shape
    group_size = HQ // HK
    kv_width = HK * DH
    score_scale = 1.0 / math.sqrt(DH)
    seq_devices = lax.axis_size("seq")
    my_start = lax.axis_index("seq") * block_len
    positions = my_start + jnp.arange(block_len, dtype=jnp.int32)
    longest = jnp.max(lengths)
    live_rows = positions[None, :] < lengths[:, None]
    query_active = my_start < longest
    inputs = tokens.reshape(-1, model_width).astype(jnp.float32)
    attn_norm, attn_pull = jax.vjp(norm_rows, inputs, gain_attn)
    attn_in = attn_norm.astype(jnp.bfloat16)
    query_pre = jnp.dot(attn_in, w_query, preferred_element_type=jnp.float32)
    query_heads = rotate(query_pre.reshape(row_count, block_len, HQ, DH), positions, 1.0).astype(
        jnp.bfloat16
    )
    query_heads = query_heads.reshape(row_count, block_len, HK, group_size, DH)
    key_pre = jnp.dot(attn_in, w_key, preferred_element_type=jnp.float32)
    key_heads = rotate(key_pre.reshape(row_count, block_len, HK, DH), positions, 1.0).astype(
        jnp.bfloat16
    )
    value_heads = jnp.dot(attn_in, w_value, preferred_element_type=jnp.float32).astype(jnp.bfloat16)
    key_value = jnp.concatenate(
        [
            key_heads.reshape(row_count, block_len, kv_width),
            value_heads.reshape(row_count, block_len, kv_width),
        ],
        axis=-1,
    )

    def allowed_for(piece_start):
        key_pos = piece_start + jnp.arange(block_len, dtype=jnp.int32)
        causal = key_pos[None, None, :] <= positions[None, :, None]
        inside = key_pos[None, None, :] < lengths[:, None, None]
        return causal & inside

    def needed_for(piece_start):
        return (piece_start <= my_start) & (piece_start < longest) & query_active

    def split_piece(pieces):
        key_part = pieces[..., :kv_width].reshape(row_count, block_len, HK, DH)
        value_part = pieces[..., kv_width:].reshape(row_count, block_len, HK, DH)
        return (key_part, value_part)

    def forward_block(carry, pieces, piece_start):

        def forward_compute_block(state):
            row_max, row_total, weighted = state
            key_part, value_part = split_piece(pieces)
            scores = (
                jnp.einsum(
                    "rqhgd,rkhd->rhgqk", query_heads, key_part, preferred_element_type=jnp.float32
                )
                * score_scale
            )
            allowed = allowed_for(piece_start)[:, None, None]
            scores = jnp.where(allowed, scores, neg_large)
            new_max = jnp.maximum(row_max, jnp.max(scores, axis=-1))
            shrink = jnp.exp(row_max - new_max)
            exp_scores = jnp.where(allowed, jnp.exp(scores - new_max[..., None]), 0.0)
            row_total = row_total * shrink + jnp.sum(exp_scores, axis=-1)
            update = jnp.einsum(
                "rhgqk,rkhd->rqhgd",
                exp_scores.astype(jnp.bfloat16),
                value_part,
                preferred_element_type=jnp.float32,
            )
            weighted = weighted * jnp.moveaxis(shrink, 3, 1)[..., None] + update
            return (new_max, row_total, weighted)

        return lax.cond(needed_for(piece_start), forward_compute_block, lambda state: state, carry)

    stat_shape = (row_count, HK, group_size, block_len)
    forward_init = (
        jnp.full(stat_shape, neg_large, jnp.float32),
        jnp.zeros(stat_shape, jnp.float32),
        jnp.zeros((row_count, block_len, HK, group_size, DH), jnp.float32),
    )
    forward_state = fold_piece(
        block_len, forward_block, forward_init, lax.all_gather(key_value, "seq", axis=1, tiled=True)
    )
    row_max, row_total, weighted = forward_state
    safe_total = jnp.where(row_total > 0, row_total, 1.0)
    attn_heads = weighted / jnp.moveaxis(safe_total, 3, 1)[..., None]
    attn_heads = jnp.where(live_rows[:, :, None, None, None], attn_heads, 0.0)
    log_sum = jnp.where(live_rows[:, None, None, :], row_max + jnp.log(safe_total), 0.0)
    attn_low = attn_heads.reshape(-1, HQ * DH).astype(jnp.bfloat16)
    residual = inputs + jnp.dot(attn_low, w_out, preferred_element_type=jnp.float32)
    ffn_norm, ffn_pull = jax.vjp(norm_rows, residual, gain_ffn)
    ffn_in = ffn_norm.astype(jnp.bfloat16)
    gate_proj = jnp.dot(ffn_in, w_gate, preferred_element_type=jnp.float32)
    up_proj = jnp.dot(ffn_in, w_up, preferred_element_type=jnp.float32)
    product, swiglu_pull = jax.vjp(
        lambda gate_in, up_in: jax.nn.silu(gate_in) * up_in, gate_proj, up_proj
    )
    hidden = product.astype(jnp.bfloat16)
    branch = jnp.dot(hidden, w_down, preferred_element_type=jnp.float32)
    mixed = (residual + branch).astype(jnp.bfloat16).reshape(row_count, block_len, model_width)
    out_low = cotangent.reshape(-1, model_width)
    out_grad = out_low.astype(jnp.float32)
    w_down_grad = inner_rows(hidden, out_low)
    hidden_grad = times_t(out_low, w_down)
    gate_grad, up_grad = swiglu_pull(hidden_grad)
    gate_low = gate_grad.astype(jnp.bfloat16)
    up_low = up_grad.astype(jnp.bfloat16)
    w_gate_grad = inner_rows(ffn_in, gate_low)
    w_up_grad = inner_rows(ffn_in, up_low)
    ffn_in_grad = times_t(gate_low, w_gate) + times_t(up_low, w_up)
    residual_part, gain_ffn_grad = ffn_pull(ffn_in_grad)
    residual_grad = out_grad + residual_part
    residual_low = residual_grad.astype(jnp.bfloat16)
    w_out_grad = inner_rows(attn_low, residual_low)
    attended_grad = times_t(residual_low, w_out).reshape(row_count, block_len, HK, group_size, DH)
    attended_grad = jnp.where(live_rows[:, :, None, None, None], attended_grad, 0.0).astype(
        jnp.bfloat16
    )
    grad_dot = jnp.moveaxis(jnp.sum(attended_grad.astype(jnp.float32) * attn_heads, axis=-1), 1, 3)

    def backward_block(with_kv, carry, pieces, piece_start):

        def backward_compute_block(state):
            key_part, value_part = split_piece(pieces)
            scores = (
                jnp.einsum(
                    "rqhgd,rkhd->rhgqk", query_heads, key_part, preferred_element_type=jnp.float32
                )
                * score_scale
            )
            allowed = allowed_for(piece_start)[:, None, None]
            weights_now = jnp.where(allowed, jnp.exp(scores - log_sum[..., None]), 0.0)
            weights_grad = jnp.einsum(
                "rqhgd,rkhd->rhgqk", attended_grad, value_part, preferred_element_type=jnp.float32
            )
            score_grad = (weights_now * (weights_grad - grad_dot[..., None])).astype(jnp.bfloat16)
            query_grad = (
                state[0]
                + jnp.einsum(
                    "rhgqk,rkhd->rqhgd", score_grad, key_part, preferred_element_type=jnp.float32
                )
                * score_scale
            )
            kv_grad = state[1]
            values_grad = jnp.einsum(
                "rhgqk,rqhgd->rkhd",
                weights_now.astype(jnp.bfloat16),
                attended_grad,
                preferred_element_type=jnp.float32,
            )
            keys_grad = (
                jnp.einsum(
                    "rhgqk,rqhgd->rkhd", score_grad, query_heads, preferred_element_type=jnp.float32
                )
                * score_scale
            )
            local_kv = jnp.concatenate(
                [
                    keys_grad.reshape(row_count, block_len, kv_width),
                    values_grad.reshape(row_count, block_len, kv_width),
                ],
                axis=-1,
            )
            current = lax.dynamic_slice_in_dim(kv_grad, piece_start, block_len, 1)
            kv_grad = lax.dynamic_update_slice_in_dim(kv_grad, current + local_kv, piece_start, 1)
            return (query_grad, kv_grad)

        return lax.cond(needed_for(piece_start), backward_compute_block, lambda state: state, carry)

    query_zero = jnp.zeros((row_count, block_len, HK, group_size, DH), jnp.float32)
    backward_init = (
        query_zero,
        jnp.zeros((row_count, block_len * seq_devices, 2 * kv_width), jnp.float32),
    )
    step_back = partial(backward_block, True)
    backward_state = fold_piece(
        block_len, step_back, backward_init, lax.all_gather(key_value, "seq", axis=1, tiled=True)
    )
    query_grad = backward_state[0]
    own_kv_grad = lax.psum_scatter(
        backward_state[1].astype(jnp.bfloat16), "seq", scatter_dimension=1, tiled=True
    ).astype(jnp.float32)
    query_low = (
        rotate(query_grad.reshape(row_count, block_len, HQ, DH), positions, -1.0)
        .astype(jnp.bfloat16)
        .reshape(-1, HQ * DH)
    )
    key_low = (
        rotate(own_kv_grad[..., :kv_width].reshape(row_count, block_len, HK, DH), positions, -1.0)
        .astype(jnp.bfloat16)
        .reshape(-1, kv_width)
    )
    value_low = own_kv_grad[..., kv_width:].astype(jnp.bfloat16).reshape(-1, kv_width)
    w_query_grad = inner_rows(attn_in, query_low)
    w_key_grad = inner_rows(attn_in, key_low)
    w_value_grad = inner_rows(attn_in, value_low)
    attn_in_grad = (
        times_t(query_low, w_query) + times_t(key_low, w_key) + times_t(value_low, w_value)
    )
    inputs_part, gain_attn_grad = attn_pull(attn_in_grad)
    tokens_grad = (
        (residual_grad + inputs_part)
        .astype(jnp.bfloat16)
        .reshape(row_count, block_len, model_width)
    )
    (
        w_query_grad,
        w_key_grad,
        w_value_grad,
        w_out_grad,
        w_gate_grad,
        w_up_grad,
        w_down_grad,
        gain_attn_grad,
        gain_ffn_grad,
    ) = lax.psum(
        (
            w_query_grad,
            w_key_grad,
            w_value_grad,
            w_out_grad,
            w_gate_grad,
            w_up_grad,
            w_down_grad,
            gain_attn_grad,
            gain_ffn_grad,
        ),
        ("dp", "seq"),
    )
    return (
        mixed,
        tokens_grad,
        w_query_grad,
        w_key_grad,
        w_value_grad,
        w_out_grad,
        w_gate_grad,
        w_up_grad,
        w_down_grad,
        gain_attn_grad,
        gain_ffn_grad,
    )


GROUP = HQ // HK
HEAD_ROWS = (GROUP + 2) * DH
SCALE = DH**-0.5
FULL = pl.BlockSpec(memory_space=pltpu.VMEM)
SMEM = pl.BlockSpec(memory_space=pltpu.SMEM)
ANY = pl.BlockSpec(memory_space=pl.ANY)


def shape_of(shape, dtype=jnp.bfloat16):
    return jax.ShapeDtypeStruct(shape, dtype)


def low(values):
    return values.astype(jnp.bfloat16)


def wide(values):
    return values.astype(jnp.float32)


def mul_nt(left, right):
    return lax.dot_general(
        left, right, (((1,), (1,)), ((), ())), preferred_element_type=jnp.float32
    )


def mul_nn(left, right):
    return lax.dot_general(
        left, right, (((1,), (0,)), ((), ())), preferred_element_type=jnp.float32
    )


class Order:
    last = None
    also = ()
    windows = False


def run(
    kernel, name, info, operands, out_shapes, scratch=(), vmem=12, grid=(), in_specs=None, out_specs=None
):
    after = [*([] if Order.last is None else [Order.last]), *Order.also]
    Order.also = ()
    taken = len(operands)

    def body(*refs):
        kernel(*refs[: 1 + taken], *refs[1 + taken + len(after) :])

    many = isinstance(out_shapes, list)
    if Order.windows and not grid:
        grid, vmem = (1,), 60
        in_specs = [once(*v.shape) for v in operands]
        out_specs = [once(*v.shape) for v in out_shapes] if many else once(*out_shapes.shape)
    outs = pl.pallas_call(
        body,
        grid=grid,
        in_specs=[SMEM] + (in_specs or [FULL] * taken) + [ANY] * len(after),
        out_specs=out_specs or ([FULL] * len(out_shapes) if many else FULL),
        scratch_shapes=list(scratch),
        out_shape=out_shapes,
        compiler_params=pltpu.CompilerParams(vmem_limit_bytes=vmem * 2**20),
        cost_estimate=pl.CostEstimate(flops=1000, bytes_accessed=1000, transcendentals=0),
        name=name,
    )(info, *operands, *after)
    Order.last = min(outs, key=lambda v: v.size) if many else outs
    return outs


def whole(*shape):
    return pl.BlockSpec(shape, lambda b: (0,) * len(shape))


def once(*shape):
    return pl.BlockSpec(shape, lambda b: (0,) * len(shape), pipeline_mode=pl.Buffered(1))


def at_block(*shape):
    return pl.BlockSpec((1, *shape), lambda b: (b, *[0] * len(shape)))


def turn(values, cosine, sine_part):
    first_half, second_half = values[: DH // 2], values[DH // 2 :]
    return jnp.concatenate(
        [
            first_half * cosine - second_half * sine_part,
            second_half * cosine + first_half * sine_part,
        ],
        axis=0,
    )


def inverse_rms(values):
    mean = jnp.sum(values * values, axis=0, keepdims=True) * (1.0 / values.shape[0])
    return lax.rsqrt(mean + eps_norm)


def norm_back(values, grad, gain):
    scale = inverse_rms(values)
    turned = grad * gain
    inner = jnp.sum(turned * values, axis=0, keepdims=True) * (1.0 / values.shape[0])
    part = scale * turned - values * (scale * scale * scale * inner)
    return part, grad * values * scale


def gain_of(ref):
    return jnp.concatenate([ref[...], ref[...]], axis=1)


def causal_mask(width):
    key_at = lax.broadcasted_iota(jnp.int32, (width, width), 0)
    query_at = lax.broadcasted_iota(jnp.int32, (width, width), 1)
    return jnp.concatenate([key_at <= query_at] * GROUP, axis=1)


def heads_of(values):
    return jnp.concatenate([values[j * DH : (j + 1) * DH] for j in range(GROUP)], axis=1)


def attend_kernel(
    info,
    row_ref,
    gain_ref,
    weights_ref,
    cos_ref,
    sin_ref,
    attn_in_ref,
    query_ref,
    key_ref,
    value_ref,
    out_ref,
    lse_ref,
    key_rows,
):
    blocks, _, width = row_ref.shape

    @pl.when(pl.program_id(0) == 0)
    def _():
        gain = gain_of(gain_ref)
        for b in range(blocks):
            values = wide(row_ref[b])
            attn_in_ref[b] = low(values * inverse_rms(values) * gain)

    mask = causal_mask(width)
    for b in range(blocks):
        pre = mul_nn(weights_ref[0], attn_in_ref[b])
        cosine, sine_part = cos_ref[b], sin_ref[b]
        for j in range(GROUP):
            query_ref[0, b, j * DH : (j + 1) * DH] = low(
                turn(pre[j * DH : (j + 1) * DH], cosine, sine_part) * SCALE
            )
        keys = low(turn(pre[GROUP * DH : (GROUP + 1) * DH], cosine, sine_part))
        key_ref[0, b] = keys
        key_rows[b] = keys.T
        value_ref[0, b] = low(pre[(GROUP + 1) * DH :])
    for b in range(blocks):
        queries = heads_of(query_ref[0, b])
        scores, top = [], None
        for k in range(b + 1):
            part = mul_nn(key_rows[k], queries)
            if k == b:
                part = jnp.where(mask, part, neg_large)
            scores.append(part)
            part_top = jnp.max(part, axis=0, keepdims=True)
            top = part_top if top is None else jnp.maximum(top, part_top)
        total, weighted = 0.0, 0.0
        for k in range(b + 1):
            weights_now = jnp.exp(scores[k] - top)
            total = total + jnp.sum(weights_now, axis=0, keepdims=True)
            weighted = weighted + mul_nn(value_ref[0, k], low(weights_now))
        weighted = weighted * (1.0 / total)
        log_sum = top + jnp.log(total)
        live = b * width + lax.broadcasted_iota(jnp.int32, (1, width), 1) < info[3]
        for j in range(GROUP):
            mine = slice(j * width, (j + 1) * width)
            out_ref[0, b, j * DH : (j + 1) * DH] = low(jnp.where(live, weighted[:, mine], 0.0))
            lse_ref[0, b, j : j + 1] = log_sum[:, mine]


def attend(info, row, gain, w_heads, cosine, sine_part):
    blocks, features, width = row.shape
    head = lambda rows: pl.BlockSpec((1, blocks, rows, width), lambda h: (h, 0, 0, 0))
    return run(
        attend_kernel,
        "attend",
        info,
        [row, gain, w_heads, cosine, sine_part],
        [
            shape_of((blocks, features, width)),
            shape_of((HK, blocks, GROUP * DH, width)),
            shape_of((HK, blocks, DH, width)),
            shape_of((HK, blocks, DH, width)),
            shape_of((HK, blocks, GROUP * DH, width)),
            shape_of((HK, blocks, 8, width), jnp.float32),
        ],
        [pltpu.VMEM((blocks, width, DH), jnp.bfloat16)],
        60,
        (HK,),
        [
            whole(*row.shape),
            whole(*gain.shape),
            pl.BlockSpec((1, HEAD_ROWS, features), lambda h: (h, 0, 0)),
            whole(*cosine.shape),
            whole(*cosine.shape),
        ],
        [whole(*row.shape), *[head(rows) for rows in (GROUP * DH, DH, DH, GROUP * DH, 8)]],
    )


def lanes_of(ref, rows=slice(None)):
    return jnp.concatenate([ref[b, rows] for b in range(ref.shape[0])], axis=1)


def put_grad(values, ref, at):
    planes, parts, _, rows, cols = ref.shape
    for p in range(planes):
        for z in range(parts):
            ref[p, z, at] = values[p * rows : (p + 1) * rows, z * cols : (z + 1) * cols].astype(
                ref.dtype
            )


CHUNK = 768


def ffn_kernel(
    info,
    row_ref,
    att_ref,
    cot_ref,
    in1_ref,
    in2_ref,
    in3_ref,
    gain_ref,
    w_out_t_ref,
    w_gate_t_ref,
    w_up_t_ref,
    w_down_t_ref,
    w_down_ref,
    w_gate_ref,
    w_up_ref,
    w_out_ref,
    mixed_ref,
    grad_ref,
    low_ref,
    att_grad_ref,
    gain_grad_ref,
    send_ref,
    keep_ref,
    ffn_ins,
    cots,
    hiddens,
    gates,
    ups,
):
    b = pl.program_id(0)
    width = row_ref.shape[2]
    gain = gain_of(gain_ref)
    attended = jnp.concatenate([att_ref[h, 0] for h in range(HK)], axis=0)
    residual = wide(row_ref[0]) + mul_nn(w_out_t_ref[...], attended)
    ffn_in = low(residual * inverse_rms(residual) * gain)
    ffn_ins[b] = ffn_in
    from_step = lax.rem(info[0] + 4 - b, 4)

    @pl.when(from_step == 0)
    def _():
        cots[b] = cot_ref[b]

    for step, ref in ((1, in1_ref), (2, in2_ref), (3, in3_ref)):

        @pl.when(from_step == step)
        def _():
            cots[b] = ref[...]

    cot = cots[b]
    mixed, ffn_in_grad = residual, 0.0
    for at in range(0, hiddens.shape[1], CHUNK):
        part = slice(at, at + CHUNK)
        gate = mul_nn(w_gate_t_ref[part], ffn_in)
        up = mul_nn(w_up_t_ref[part], ffn_in)
        hidden_grad = mul_nn(w_down_ref[part], cot)
        sigmoid = 1.0 / (1.0 + jnp.exp(-gate))
        silu = gate * sigmoid
        hidden = low(silu * up)
        gate_grad = low(hidden_grad * up * (sigmoid + silu * (1.0 - sigmoid)))
        up_grad = low(hidden_grad * silu)
        hiddens[b, part] = hidden
        gates[b, part] = gate_grad
        ups[b, part] = up_grad
        mixed = mixed + mul_nn(w_down_t_ref[:, part], hidden)
        ffn_in_grad = ffn_in_grad + (
            mul_nn(w_gate_ref[:, part], gate_grad) + mul_nn(w_up_ref[:, part], up_grad)
        )
    mixed_ref[0] = low(mixed)
    part, gain_terms = norm_back(residual, ffn_in_grad, gain)
    gain_terms = gain_terms[:, : width // 2] + gain_terms[:, width // 2 :]

    @pl.when(b == 0)
    def _():
        gain_grad_ref[...] = gain_terms

    @pl.when(b > 0)
    def _():
        gain_grad_ref[...] += gain_terms

    grad = wide(cot) + part
    grad_ref[0] = grad
    grad_low = low(grad)
    low_ref[0] = grad_low
    live = b * width + lax.broadcasted_iota(jnp.int32, (1, width), 1) < info[3]
    att_grad_ref[0] = low(jnp.where(live, mul_nn(w_out_ref[...], grad_low), 0.0))

    @pl.when(b == pl.num_programs(0) - 1)
    def _():
        rows = grad_ref.shape[1] // 2
        for half, ref in ((1 - info[1], send_ref), (info[1], keep_ref)):
            own = pl.ds(pl.multiple_of(half * rows, 16), rows)
            left = lanes_of(ffn_ins, own)
            put_grad(mul_nt(left, lanes_of(gates)), ref, 0)
            put_grad(mul_nt(left, lanes_of(ups)), ref, 1)
            put_grad(mul_nt(lanes_of(cots, own), lanes_of(hiddens)), ref, 2)


def ffn(info, row, attended, cot, arrived, gain, turned, straight):
    blocks, features, width = row.shape
    hidden = turned[1].shape[0]
    block, long = (blocks, features, width), (blocks, hidden, width)
    pieces = (4, 4, 3, features // 8, hidden // 4)
    return run(
        ffn_kernel,
        "ffn",
        info,
        [row, attended, cot, *arrived, gain, *turned, *straight],
        [
            shape_of(block),
            shape_of(block, jnp.float32),
            shape_of(block),
            shape_of(block),
            shape_of(gain.shape, jnp.float32),
            shape_of(pieces),
            shape_of(pieces),
        ],
        [pltpu.VMEM(block, jnp.bfloat16)] * 2 + [pltpu.VMEM(long, jnp.bfloat16)] * 3,
        52,
        (blocks,),
        [
            at_block(features, width),
            pl.BlockSpec((HK, 1, GROUP * DH, width), lambda b: (0, b, 0, 0)),
            whole(*cot.shape),
            *[whole(features, width)] * 3,
            whole(*gain.shape),
            *[FULL] * 8,
        ],
        [
            *[at_block(features, width)] * 4,
            whole(*gain.shape),
            *[whole(*pieces)] * 2,
        ],
    )


PIECE_ROWS = 48
PIECE_COLS = 640


def attend_back(refs, grad_ref, scratch):
    query_ref, key_ref, value_ref, out_ref, out_grad_ref, lse_ref, cos_ref, sin_ref = refs
    key_rows, value_rows, key_sum, value_sum = scratch
    blocks, width = query_ref.shape[1], query_ref.shape[3]
    for b in range(blocks):
        key_rows[b] = key_ref[0, b].T
        value_rows[b] = value_ref[0, b].T
    mask = causal_mask(width)
    for b in reversed(range(blocks)):
        queries, out_grad = heads_of(query_ref[0, b]), heads_of(out_grad_ref[b])
        grad_dot = jnp.sum(wide(out_grad) * wide(heads_of(out_ref[0, b])), axis=0, keepdims=True)
        log_sum = jnp.concatenate([lse_ref[0, b, j : j + 1] for j in range(GROUP)], axis=1)
        query_grad = 0.0
        for k in range(b + 1):
            weights_now = jnp.exp(mul_nn(key_rows[k], queries) - log_sum)
            if k == b:
                weights_now = jnp.where(mask, weights_now, 0.0)
            weights_grad = mul_nn(value_rows[k], out_grad)
            score_grad = low(weights_now * (weights_grad - grad_dot))
            value_part = mul_nt(out_grad, low(weights_now))
            key_part = mul_nt(queries, score_grad)
            if b == blocks - 1:
                value_sum[k] = value_part
                key_sum[k] = key_part
            else:
                value_sum[k] += value_part
                key_sum[k] += key_part
            query_grad = query_grad + mul_nn(key_ref[0, k], score_grad)
        cosine, sine_part = cos_ref[b], -sin_ref[b]
        for j in range(GROUP):
            grad_ref[b, j * DH : (j + 1) * DH] = low(
                turn(query_grad[:, j * width : (j + 1) * width], cosine * SCALE, sine_part * SCALE)
            )
        grad_ref[b, GROUP * DH : (GROUP + 1) * DH] = low(turn(key_sum[b], cosine, sine_part))
        grad_ref[b, (GROUP + 1) * DH :] = low(value_sum[b])


def back_kernel(info, *refs):
    heads, refs = refs[:8], refs[8:]
    (gain_ref, gain_ffn_ref), far, refs = refs[:2], refs[2:8], refs[8:]
    (out_ref, send_ref, keep_ref), refs = refs[:3], refs[3:]
    qkv_ref, gain_sum, scratch, near, sems = refs[0], refs[1], refs[2:6], refs[6:12], refs[12]
    row_ref, grad_ref, w_ref, attn_in_ref, att_ref, low_ref = near
    h = pl.program_id(0)
    copies = [
        pltpu.make_async_copy(there, here, sems.at[k])
        for k, (there, here) in enumerate(zip(far, near))
    ]

    @pl.when(h == 0)
    def _():
        for copy in copies:
            copy.start()

    attend_back(heads, qkv_ref.at[h], scratch)

    @pl.when(h == HK - 1)
    def _():
        for copy in copies:
            copy.wait()
        tokens_back(row_ref, grad_ref, gain_ref, w_ref, qkv_ref, out_ref, gain_sum)
        first = lambda ref: attn_grad_first(qkv_ref, attn_in_ref, gain_sum, gain_ffn_ref, ref)
        second = lambda ref: attn_grad_second(qkv_ref, attn_in_ref, att_ref, low_ref, ref)

        @pl.when(info[1] == 0)
        def _():
            second(send_ref)
            first(keep_ref)

        @pl.when(info[1] == 1)
        def _():
            first(send_ref)
            second(keep_ref)


def tokens_back(row_ref, grad_ref, gain_ref, w_ref, qkv_ref, out_ref, gain_sum):
    width = row_ref.shape[2]
    gain = gain_of(gain_ref)
    gain_sum[...] = jnp.zeros_like(gain_sum)

    def one_block(b, carry):
        qkv = jnp.concatenate([qkv_ref[h, b] for h in range(HK)], axis=0)
        part, gain_terms = norm_back(wide(row_ref[b]), mul_nn(w_ref[...], qkv), gain)
        gain_sum[...] += gain_terms[:, : width // 2] + gain_terms[:, width // 2 :]
        out_ref[b] = low(grad_ref[b] + part)
        return carry

    lax.fori_loop(0, row_ref.shape[0], one_block, 0)


def put_rows(values, ref, at, columns=None):
    features = values.shape[1]
    if columns is None:
        columns = jnp.zeros((values.shape[0], PIECE_COLS - features), jnp.float32)
    for piece in range(values.shape[0] // PIECE_ROWS):
        rows = slice(piece * PIECE_ROWS, (piece + 1) * PIECE_ROWS)
        p, z = (at + piece) // 4, (at + piece) % 4
        ref[p, z, 0, :, :features] = values[rows].astype(ref.dtype)
        ref[p, z, 0, :, features:] = columns[rows].astype(ref.dtype)


def take_rows(qkv_ref, start, size):
    rows = slice(start, start + size)
    return jnp.concatenate([lanes_of(qkv_ref.at[h], rows) for h in range(HK)], axis=0)


def attn_grad_first(qkv_ref, attn_in_ref, gain1_ref, gain2_ref, ref):
    attn_in = lanes_of(attn_in_ref)
    features = attn_in.shape[0]
    lane = lax.broadcasted_iota(jnp.int32, (features, PIECE_COLS - features), 1)
    gains = jnp.where(
        lane == 0,
        jnp.sum(gain1_ref[...], axis=1, keepdims=True),
        jnp.where(lane == 1, jnp.sum(gain2_ref[...], axis=1, keepdims=True), 0.0),
    )
    put_rows(mul_nt(attn_in, take_rows(qkv_ref, 0, GROUP * DH)), ref, 0, gains)
    keys = take_rows(qkv_ref, GROUP * DH, DH)
    put_rows(mul_nt(keys, attn_in), ref, features // PIECE_ROWS)


def attn_grad_second(qkv_ref, attn_in_ref, att_ref, low_ref, ref):
    values = take_rows(qkv_ref, (GROUP + 1) * DH, DH)
    put_rows(mul_nt(values, lanes_of(attn_in_ref)), ref, 0)
    attended = jnp.concatenate([lanes_of(att_ref.at[h]) for h in range(HK)], axis=0)
    put_rows(mul_nt(attended, lanes_of(low_ref)), ref, HK * DH // PIECE_ROWS)


def back(info, heads, attended_grad, log_sum, angles, gains, rest):
    queries, keys, values, attended = heads
    row = rest[0]
    _, blocks, _, width = queries.shape
    head = lambda rows: pl.BlockSpec((1, blocks, rows, width), lambda h: (h, 0, 0, 0))
    angle = once(*angles[0].shape)
    pieces = (4, 4, 1, PIECE_ROWS, PIECE_COLS)
    return run(
        back_kernel,
        "back",
        info,
        [queries, keys, values, attended, attended_grad, log_sum, *angles, *gains, *rest],
        [shape_of(row.shape), shape_of(pieces), shape_of(pieces)],
        [
            pltpu.VMEM((HK, blocks, HEAD_ROWS, width), jnp.bfloat16),
            pltpu.VMEM(gains[0].shape, jnp.float32),
        ]
        + [pltpu.VMEM((blocks, width, DH), jnp.bfloat16)] * 2
        + [pltpu.VMEM((blocks, DH, width), jnp.float32)] * 2
        + [pltpu.VMEM(v.shape, v.dtype) for v in rest]
        + [pltpu.SemaphoreType.DMA((6,))],
        60,
        (HK,),
        [
            *[head(rows) for rows in (GROUP * DH, DH, DH, GROUP * DH)],
            pl.BlockSpec((blocks, GROUP * DH, width), lambda h: (0, h, 0)),
            head(8),
            angle,
            angle,
            *[once(*g.shape) for g in gains],
            *[ANY] * 6,
        ],
        [whole(*row.shape), whole(*pieces), whole(*pieces)],
    )


def bit_of(value, bit):
    return lax.rem(value // (1 << bit), 2)


def plane_at(first, own, other):
    return own + 2 * other if first == 0 else other + 2 * own


def spot(routes, near, far):
    if len(routes) == 1:
        return 0, near + 2 * far
    return far, near


def split_plane_kernel(routes, info, keep_ref, in_ref, *outs):
    for k, (first, places) in enumerate(routes):
        mine = bit_of(info[2], first)
        send_ref, own_ref = outs[2 * k : 2 * k + 2]
        for t in range(2):
            there, here = plane_at(first, 1 - mine, t), plane_at(first, mine, t)
            for at, z in enumerate(places):
                send_ref[t, at] = low(wide(keep_ref[there, z]) + wide(in_ref[there, z]))
                own_ref[t, at] = wide(keep_ref[here, z]) + wide(in_ref[here, z])


def split_line_kernel(routes, info, *refs):
    count = len(routes)
    ins, outs = refs[: 2 * count], refs[2 * count :]
    for k, (first, _) in enumerate(routes):
        mine = bit_of(info[2], 1 - first)
        keep_ref, in_ref = ins[2 * k : 2 * k + 2]
        send_ref, own_ref = outs[2 * k : 2 * k + 2]
        send_ref[...] = low(keep_ref[1 - mine] + wide(in_ref[1 - mine]))
        own_ref[...] = keep_ref[mine] + wide(in_ref[mine])


def split_near_kernel(routes, info, *refs):
    ins, (send_ref, own_ref) = refs[:-2], refs[-2:]
    near = bit_of(info[0], 0)
    for far in range(2):
        k, there = spot(routes, 1 - near, far)
        k, here = spot(routes, near, far)
        keep_ref, in_ref = ins[2 * k : 2 * k + 2]
        send_ref[far] = low(keep_ref[there] + wide(in_ref[there]))
        own_ref[far] = keep_ref[here] + wide(in_ref[here])


def split_far_kernel(routes, info, keep_ref, in_ref, send_ref, own_ref):
    far = bit_of(info[0], 1)
    send_ref[...] = low(keep_ref[1 - far] + wide(in_ref[1 - far]))
    own_ref[...] = keep_ref[far] + wide(in_ref[far])


def total_kernel(routes, info, keep_ref, in_ref, out_ref):
    out_ref[...] = low(keep_ref[...] + wide(in_ref[...]))


def join_far_kernel(routes, info, own_ref, in_ref, out_ref):
    far = bit_of(info[0], 1)
    out_ref[far] = own_ref[...]
    out_ref[1 - far] = in_ref[...]


def join_near_kernel(routes, info, own_ref, in_ref, *outs):
    near = bit_of(info[0], 0)
    for far in range(2):
        k, here = spot(routes, near, far)
        k, there = spot(routes, 1 - near, far)
        outs[k][here] = own_ref[far]
        outs[k][there] = in_ref[far]


def join_line_kernel(routes, info, *refs):
    count = len(routes)
    ins, outs = refs[: 2 * count], refs[2 * count :]
    for k, (first, _) in enumerate(routes):
        mine = bit_of(info[2], 1 - first)
        outs[k][mine] = ins[2 * k][...]
        outs[k][1 - mine] = ins[2 * k + 1][...]


def join_plane_kernel(routes, info, *refs):
    ins, out_ref = refs[:-1], refs[-1]
    for k, (first, places) in enumerate(routes):
        mine = bit_of(info[2], first)
        own_ref, in_ref = ins[2 * k : 2 * k + 2]
        for t in range(2):
            for at, z in enumerate(places):
                out_ref[plane_at(first, mine, t), z] = own_ref[t, at]
                out_ref[plane_at(first, 1 - mine, t), z] = in_ref[t, at]


def swap(values, axis, bits):
    count = 8 if axis == "dp" else 4
    return lax.ppermute(values, axis, [(k, k ^ bits) for k in range(count)])


TWO_ROUTES = ((0, (0, 1)), (1, (2, 3)))


class Sum:
    def __init__(self, info, send_keep, routes):
        self.info, self.routes = info, routes
        self.send, self.keep = send_keep
        self.piece = self.send.shape[2:]
        self.stage = 0
        self.next = swap(self.send, "dp", 1)

    def call(self, kernel, operands, shapes):
        return run(partial(kernel, self.routes), kernel.__name__[:-7], self.info, operands, shapes)

    def step(self):
        routes, piece = self.routes, tuple(self.piece)
        count, places = len(routes), len(routes[0][1])
        both = lambda *shape: [shape_of(shape), shape_of(shape, jnp.float32)]
        plane = [2 << first for first, _ in routes]
        line = [2 << (1 - first) for first, _ in routes]
        if self.stage == 0:
            self.outs = self.call(
                split_plane_kernel, [self.keep, self.next], both(2, places, *piece) * count
            )
            self.next = [swap(self.outs[2 * k], "dp", plane[k]) for k in range(count)]
        elif self.stage in (1, 2):
            operands = []
            for k in range(count):
                operands += [self.outs[2 * k + 1], self.next[k]]
            if self.stage == 1:
                self.outs = self.call(split_line_kernel, operands, both(places, *piece) * count)
                self.next = [swap(self.outs[2 * k], "dp", line[k]) for k in range(count)]
            else:
                self.outs = self.call(split_near_kernel, operands, both(2, *piece))
                self.next = swap(self.outs[0], "seq", 1)
        elif self.stage == 3:
            self.outs = self.call(split_far_kernel, [self.outs[1], self.next], both(*piece))
            self.next = swap(self.outs[0], "seq", 2)
        elif self.stage == 4:
            self.outs = self.call(total_kernel, [self.outs[1], self.next], shape_of(piece))
            self.next = swap(self.outs, "seq", 2)
        elif self.stage == 5:
            self.outs = self.call(join_far_kernel, [self.outs, self.next], shape_of((2, *piece)))
            self.next = swap(self.outs, "seq", 1)
        elif self.stage == 6:
            self.outs = self.call(
                join_near_kernel, [self.outs, self.next], [shape_of((places, *piece))] * count
            )
            self.next = [swap(self.outs[k], "dp", line[k]) for k in range(count)]
        elif self.stage in (7, 8):
            operands = []
            for k in range(count):
                operands += [self.outs[k], self.next[k]]
            if self.stage == 7:
                self.outs = self.call(
                    join_line_kernel, operands, [shape_of((2, places, *piece))] * count
                )
                self.next = [swap(self.outs[k], "dp", plane[k]) for k in range(count)]
            else:
                self.outs = self.call(join_plane_kernel, operands, shape_of((4, 4, *piece)))
                self.next = swap(self.outs, "dp", 1)
        self.stage += 1


def add_core_kernel(info, keep_ref, in_ref, own_ref, *out_refs):
    plane = info[2]
    own_ref[...] = wide(keep_ref[plane]) + wide(in_ref[plane])
    for step, ref in enumerate(out_refs):
        other = plane ^ (step + 1)
        ref[...] = low(wide(keep_ref[other]) + wide(in_ref[other]))


def add_plane_kernel(info, keep_ref, in1_ref, in2_ref, in3_ref, own_ref, *out_refs):
    total = lambda z: (
        (keep_ref[z] + wide(in1_ref[z])) + (wide(in2_ref[z]) + wide(in3_ref[z]))
    )
    own_ref[...] = total(info[0])
    for step, ref in enumerate(out_refs):
        ref[...] = low(total(lax.rem(info[0] + step + 1, 4)))


def add_seq_kernel(info, keep_ref, in1_ref, in2_ref, in3_ref, out_ref):
    out_ref[...] = low(
        (keep_ref[...] + wide(in1_ref[...])) + (wide(in2_ref[...]) + wide(in3_ref[...]))
    )


def join_seq_kernel(info, own_ref, in1_ref, in2_ref, in3_ref, out_ref):
    for step, ref in enumerate((own_ref, in1_ref, in2_ref, in3_ref)):
        out_ref[lax.rem(info[0] + 4 - step, 4)] = ref[...]


def join_chips_kernel(info, own_ref, in1_ref, in2_ref, in3_ref, out_ref):
    for step, ref in enumerate((own_ref, in1_ref, in2_ref, in3_ref)):
        out_ref[info[2] ^ step] = ref[...]


class DirectSum:
    def __init__(self, info, send_keep):
        self.info = info
        self.send, self.keep = send_keep
        self.piece = self.send.shape[2:]
        self.stage = 0
        self.next = [swap(self.send, "dp", 1)]

    def step(self):
        piece = tuple(self.piece)
        line = (4, *piece)
        kernel, shapes = [
            (add_core_kernel, [shape_of(line, jnp.float32)] + [shape_of(line)] * 3),
            (add_plane_kernel, [shape_of(piece, jnp.float32)] + [shape_of(piece)] * 3),
            (add_seq_kernel, shape_of(piece)),
            (join_seq_kernel, shape_of(line)),
            (join_chips_kernel, shape_of((4, *line))),
        ][self.stage]
        first = self.keep if self.stage == 0 else self.outs
        if isinstance(first, list | tuple):
            first = first[0]
        outs = run(kernel, kernel.__name__[:-7], self.info, [first, *self.next], shapes)
        self.outs = outs
        sends = outs[1:] if isinstance(outs, list | tuple) else [outs] * 3
        if self.stage in (0, 3):
            self.next = [swap(v, "dp", 2 * k) for k, v in zip((1, 2, 3), sends)]
        elif self.stage in (1, 2):
            self.next = [shift(v, k) for k, v in zip((1, 2, 3), sends)]
        else:
            self.next = [swap(outs, "dp", 1)]
        self.stage += 1


def join_wide_kernel(info, own_ref, in_ref, *out_refs):
    _, parts, count, rows, cols = own_ref.shape
    for ref, core in ((own_ref, info[1]), (in_ref, 1 - info[1])):
        for z in range(parts):
            for k in range(count):
                out_refs[k][core, 0, :, z * cols : (z + 1) * cols] = wide(ref[0, z, k])


def join_wide(info, own, came):
    _, parts, count, rows, cols = own.shape
    piece = pl.BlockSpec((1, parts, count, rows, cols), lambda p: (p, 0, 0, 0, 0))
    outs = run(
        join_wide_kernel,
        "join",
        info,
        [own, came],
        [shape_of((2, 4, rows, parts * cols), jnp.float32)] * count,
        [],
        16,
        (4,),
        [piece] * 2,
        [pl.BlockSpec((2, 1, rows, parts * cols), lambda p: (0, p, 0, 0))] * count,
    )
    return [v.reshape(8 * rows, parts * cols) for v in outs]


def join_attn_kernel(
    info, own_ref, in_ref, query_ref, key_ref, value_ref, out_ref, gains_ref, total
):
    planes, parts, _, rows, cols = own_ref.shape
    for ref, core in ((own_ref, info[1]), (in_ref, 1 - info[1])):
        for p in range(planes):
            for z in range(parts):
                total[core * (planes * parts) + p * parts + z] = wide(ref[p, z, 0])
    at = 0
    features = query_ref.shape[1]
    for ref in (query_ref, key_ref, value_ref, out_ref):
        for piece in range(ref.shape[0] // rows):
            ref[piece * rows : (piece + 1) * rows] = total[at, :, :features]
            if ref is query_ref:
                gains_ref[piece * rows : (piece + 1) * rows] = total[at, :, cols - 128 :]
            at += 1


def cut_kernel(info, values_ref, *refs):
    outs, sems = refs[:-1], refs[-1]
    copies = [
        pltpu.make_async_copy(values_ref.at[lax.rem(info[0] + step + 1, 4)], out, sems.at[step])
        for step, out in enumerate(outs)
    ]
    for copy in copies:
        copy.start()
    for copy in copies:
        copy.wait()


def cut(info, values):
    return run(
        cut_kernel,
        "cut",
        info,
        [values],
        [shape_of(values.shape[1:])] * 3,
        [pltpu.SemaphoreType.DMA((3,))],
        12,
        (1,),
        [ANY],
        [ANY] * 3,
    )


def shift(values, step):
    return lax.ppermute(values, "seq", [(k, (k + step) % 4) for k in range(4)])


def place_kernel(info, in_ref, out_ref):
    out_ref[...] = in_ref[...]


def place(info, values):
    return run(place_kernel, "place", info, [values], shape_of(values.shape))


def exchange(values):
    return lax.all_to_all(values, "seq", 0, 0)


def local_rows(
    tokens,
    lengths,
    w_query,
    w_key,
    w_value,
    w_out,
    w_gate,
    w_up,
    w_down,
    gain_attn,
    gain_ffn,
    cotangent,
):
    row_count, block_len, model_width = tokens.shape
    kv_width = HK * DH
    dp_at, seq_at = lax.axis_index("dp"), lax.axis_index("seq")
    length = lax.dynamic_slice_in_dim(lengths, seq_at, 1)
    info = jnp.concatenate([jnp.stack([seq_at, dp_at % 2, dp_at // 2]).astype(jnp.int32), length])
    half_dim = DH // 2
    positions = jnp.arange(row_count * block_len, dtype=jnp.float32).reshape(row_count, 1, -1)
    frequency = rope_base ** (-jnp.arange(half_dim, dtype=jnp.float32) / half_dim)
    angles = frequency[None, :, None] * positions
    angles = (jnp.cos(angles), jnp.sin(angles))
    w_heads = jnp.concatenate(
        [
            w_query.T.reshape(HK, GROUP * DH, model_width),
            w_key.T.reshape(HK, DH, model_width),
            w_value.T.reshape(HK, DH, model_width),
        ],
        axis=1,
    )
    w_heads_t = w_heads.reshape(-1, model_width).T
    gains = [
        jnp.broadcast_to(g[:, None], (model_width, block_len // 2)) for g in (gain_attn, gain_ffn)
    ]
    turned = [w_out.T, w_gate.T, w_up.T, w_down.T]

    row = exchange(jnp.swapaxes(tokens, 1, 2))
    cot, info, w_heads, w_heads_t, gains, angles, turned, w_down = lax.optimization_barrier(
        (
            jnp.swapaxes(cotangent, 1, 2),
            info,
            w_heads,
            w_heads_t,
            gains,
            angles,
            turned,
            w_down,
        )
    )
    Order.last, Order.also, Order.windows = None, (), False
    arrived = [shift(part, s + 1) for s, part in enumerate(cut(info, cot))]
    attn_in, queries, keys, values, attended, log_sum = attend(info, row, gains[0], w_heads, *angles)
    mixed, grad, grad_low, attended_grad, gain_ffn_part, *halves = ffn(
        info, row, attended, cot, arrived, gains[1], turned, [w_down, w_gate, w_up, w_out]
    )
    wide_sum = Sum(info, halves, TWO_ROUTES)
    Order.windows = True

    mixed_out = exchange(mixed)
    wide_sum.step()
    tokens_grad, *halves = back(
        info,
        (queries, keys, values, attended),
        attended_grad,
        log_sum,
        angles,
        (gains[0], gain_ffn_part),
        (row, grad, w_heads_t, attn_in, attended, grad_low),
    )
    wide_sum.step()
    Order.windows = False
    halves, Order.last = lax.optimization_barrier((halves, Order.last))
    attn_sum = DirectSum(info, halves)
    attn_sum.step()
    Order.also = (mixed_out,)
    wide_sum.step()
    wide_sum.step()
    attn_sum.step()
    wide_sum.step()
    attn_sum.step()
    wide_sum.step()
    attn_sum.step()
    wide_sum.step()
    tokens_grad, Order.last = lax.optimization_barrier((tokens_grad, Order.last))
    tokens_out = exchange(tokens_grad)
    Order.windows = True
    wide_sum.step()
    attn_sum.step()
    square = shape_of((model_width, model_width), jnp.float32)
    narrow = shape_of((kv_width, model_width), jnp.float32)
    shapes = [square, narrow, narrow, square, shape_of((model_width, 128), jnp.float32)]
    w_query_sum, w_key_sum, w_value_sum, w_out_sum, gains_sum = run(
        join_attn_kernel,
        "join",
        info,
        [attn_sum.outs, *attn_sum.next],
        shapes,
        [pltpu.VMEM((32, PIECE_ROWS, PIECE_COLS), jnp.float32)],
        24,
        (1,),
        [once(*attn_sum.outs.shape)] * 2,
        [once(*v.shape) for v in shapes],
    )
    mixed_out = place(info, mixed_out)
    Order.also = (tokens_out,)
    wide_sum.step()
    tokens_out = place(info, tokens_out)
    w_gate_sum, w_up_sum, w_down_sum = join_wide(info, wide_sum.outs, wide_sum.next)
    return (
        jnp.swapaxes(mixed_out, 1, 2),
        jnp.swapaxes(tokens_out, 1, 2),
        w_query_sum,
        w_key_sum.T,
        w_value_sum.T,
        w_out_sum,
        w_gate_sum,
        w_up_sum,
        w_down_sum.T,
        gains_sum[:, 64],
        gains_sum[:, 65],
    )


def solution(mesh):
    whole_rows = mesh.shape["dp"] == 8 and mesh.shape["seq"] == 4
    return jax.shard_map(
        local_rows if whole_rows else local_general,
        mesh=mesh,
        in_specs=(
            P("dp", "seq", None),
            P("dp"),
            P(),
            P(),
            P(),
            P(),
            P(),
            P(),
            P(),
            P(),
            P(),
            P("dp", "seq", None),
        ),
        out_specs=(
            P("dp", "seq", None),
            P("dp", "seq", None),
            P(),
            P(),
            P(),
            P(),
            P(),
            P(),
            P(),
            P(),
            P(),
        ),
        check_vma=False,
    )
```

profile of v0, /device:TPU:0, one launch (start us, length us, event | category | flops | bytes accessed | tf_op | source)
XLA Modules:
  0.0 266.8 jit_solution(4507749973576593973)
XLA Ops:
  0.7 6.5 %all-to-all-start = ((bf16[4,576,256]{2,1,0:T(8,128)(2,1)}), bf16[4,576,256]{2,1,0:T(8,128)(2,1)}, u32[]{:S(2)}, u32[]{:S(2)}) async-start(bf16[4,576,256]{2,1,0:T(8,128)(2,1)} %bitcast.39), calls=%async_computation | async-start | bytes 2359296 | tf_op jit(solution)/shard_map/all_to_all | solution.py:1161
  13.4 4.0 %copy.33 = bf16[576,1536]{0,1:T(8,128)(2,1)} copy(bf16[576,1536]{1,0:T(8,128)(2,1)} %refs_14_.1) | data formatting | bytes 3538944 | tf_op args[7]
  21.8 3.0 %collective-permute-start.1 = (bf16[576,256]{1,0:T(8,128)(2,1)S(1)}, bf16[576,256]{1,0:T(8,128)(2,1)S(1)}, u32[]{:S(2)}, u32[]{:S(2)}) collective-permute-start(bf16[576,256]{1,0:T(8,128)(2,1)S(1)} %get-tuple-element.88), channel_id=1, source_target_pairs={{0,2},{1,3},{2,0},{3,1},{4,6},{5,7},{6,4},{7,5},{8,10},{9,11},{10,... | collective-permute-start | bytes 884744 | tf_op jit(solution)/shard_map/ppermute | solution.py:1149
  26.8 3.9 %copy.34.refs_12_ = bf16[1536,576]{1,0:T(8,128)(2,1)} copy(bf16[1536,576]{0,1:T(8,128)(2,1)} %param.20) | data formatting | bytes 3538944 | tf_op jit(solution)/shard_map/optimization_barrier | solution.py:1203
  30.7 13.9 %all-to-all-done.refs_1_.refs_11_ = bf16[4,576,256]{2,1,0:T(8,128)(2,1)} async-done(((bf16[4,576,256]{2,1,0:T(8,128)(2,1)}), bf16[4,576,256]{2,1,0:T(8,128)(2,1)}, u32[]{:S(2)}, u32[]{:S(2)}) %all-to-all-start) | async-done | bytes 1179680 | tf_op jit(solution)/shard_map/all_to_all | solution.py:1161
  44.6 14.4 %attend.1 = (bf16[4,576,256]{2,1,0:T(8,128)(2,1)}, bf16[3,4,192,256]{3,2,1,0:T(8,128)(2,1)}, bf16[3,4,64,256]{3,2,1,0:T(8,128)(2,1)}, bf16[3,4,64,256]{3,2,1,0:T...) custom-call(s32[4]{0:T(128)} %copy-done.17, ...), custom_call_target="tpu_custom_call" | custom-call | flops 1000 | bytes 1000 | tf_op jit(solution)/shard_map/attend/pallas_call | solution.py:376
  59.9 35.7 %ffn.1 = (bf16[4,576,256]{2,1,0:T(8,128)(2,1)}, f32[4,576,256]{2,1,0:T(8,128)}, bf16[4,576,256]{2,1,0:T(8,128)(2,1)}, bf16[4,576,256]{2,1,0:T(8,128)(2,1)}, f32[...) custom-call(s32[4]{0:T(128)S(1)} %copy-done.18, ...), custom_call_target="tpu_custom_call" | custom-call | flops 1000 | bytes 1000 | tf_op jit(solution)/shard_map/ffn/pallas_call | solution.py:376
  96.3 8.0 %all-to-all-start.1 = ((bf16[4,576,256]{2,1,0:T(8,128)(2,1)}), bf16[4,576,256]{2,1,0:T(8,128)(2,1)S(1)}, u32[]{:S(2)}, u32[]{:S(2)}) async-start(bf16[4,576,256]{2,1,0:T(8,128)(2,1)} %get-tuple-element.97), calls=%async_computation.1 | async-start | bytes 2359296 | tf_op jit(solution)/shard_map/all_to_all | solution.py:1161
  104.4 4.6 %split_plane.1 = (bf16[2,2,3,72,384]{4,3,2,1,0:T(8,128)(2,1)}, f32[2,2,3,72,384]{4,3,2,1,0:T(8,128)}, bf16[2,2,3,72,384]{4,3,2,1,0:T(8,128)(2,1)}, f32[2,2,3,72,384]{4,3,2,1,0:T(8,128)}) custom-call(s32[4]{0:T(128)} %copy-done.17, bf16[4,4,3,72,384]{4,3,2,1,0:T(8,128)(2,1)} %get-tuple-element.107.refs_1_, ...), custom_call_target="tpu_custom_call" | custom-call | flops 1000 | bytes 1000 | tf_op jit(solution)/shard_map/split_plane/pallas_call | solution.py:376
  112.0 23.9 %back.1 = (bf16[4,576,256]{2,1,0:T(8,128)(2,1)}, bf16[4,4,1,48,640]{4,3,2,1,0:T(8,128)(2,1)}, bf16[4,4,1,48,640]{4,3,2,1,0:T(8,128)(2,1)}) custom-call(s32[4]{0:T(128)} %copy-done.17, bf16[3,4,192,256]{3,2,1,0:T(8,128)(2,1)} %get-tuple-element.98.refs_1_, bf16[3,4,64,256]{3,2,1,0:T(8,128)(2,1)} %get-tuple-element.99.refs_2_, ...), custom_call_target="tpu_custom_call" | custom-call | flops 1000 | bytes 1000 | tf_op jit(solution)/shard_map/back/pallas_call | solution.py:376
  137.0 3.7 %split_line.1 = (bf16[2,3,72,384]{3,2,1,0:T(8,128)(2,1)}, f32[2,3,72,384]{3,2,1,0:T(8,128)}, bf16[2,3,72,384]{3,2,1,0:T(8,128)(2,1)}, f32[2,3,72,384]{3,2,1,0:T(8,128)}) custom-call(s32[4]{0:T(128)} %copy-done.17, f32[2,2,3,72,384]{4,3,2,1,0:T(8,128)} %get-tuple-element.112.refs_1_, bf16[2,2,3,72,384]{4,3,2,1,0:T(8,128)(2,1)} %copy-done.35, ...), custom_call_target="tpu_custom_call" | custom-call | flops 1000 | bytes 1000 | tf_op jit(solution)/shard_map/split_line/pallas_call | solution.py:376
  147.3 3.9 %collective-permute-done.11.refs_4_ = bf16[2,3,72,384]{3,2,1,0:T(8,128)(2,1)} collective-permute-done((bf16[2,3,72,384]{3,2,1,0:T(8,128)(2,1)}, bf16[2,3,72,384]{3,2,1,0:T(8,128)(2,1)}, u32[]{:S(2)}, u32[]{:S(2)}) %collective-permute-start.11) | collective-permute-done | bytes 331808 | tf_op jit(solution)/shard_map/ppermute | solution.py:944
  159.4 3.9 %collective-permute-done.12.refs_2_ = bf16[2,3,72,384]{3,2,1,0:T(8,128)(2,1)S(1)} collective-permute-done((bf16[2,3,72,384]{3,2,1,0:T(8,128)(2,1)S(1)}, bf16[2,3,72,384]{3,2,1,0:T(8,128)(2,1)S(1)}, u32[]{:S(2)}, u32[]{:S(2)}) %collective-permute-start.12) | collective-permute-done | bytes 331808 | tf_op jit(solution)/shard_map/ppermute | solution.py:944
  164.0 2.7 %collective-permute-start.16 = (bf16[3,72,384]{2,1,0:T(8,128)(2,1)S(1)}, bf16[3,72,384]{2,1,0:T(8,128)(2,1)S(1)}, u32[]{:S(2)}, u32[]{:S(2)}) collective-permute-start(bf16[3,72,384]{2,1,0:T(8,128)(2,1)S(1)} %get-tuple-element.128.refs_5_), channel_id=1, source_target_pairs={{0,2},{1,3},{2,0},{3,1},{4,6},{5,7},{6,4},{7,5},{8,10},{9,11},{10,... | collective-permute-start | bytes 497672 | tf_op jit(solution)/shard_map/ppermute | solution.py:944
  166.7 2.7 %collective-permute-done.8.refs_3_ = bf16[4,1,48,640]{3,2,1,0:T(8,128)(2,1)S(1)} collective-permute-done((bf16[4,1,48,640]{3,2,1,0:T(8,128)(2,1)S(1)}, bf16[4,1,48,640]{3,2,1,0:T(8,128)(2,1)S(1)}, u32[]{:S(2)}, u32[]{:S(2)}) %collective-permute-start.8) | collective-permute-done | bytes 245792 | tf_op jit(solution)/shard_map/ppermute | solution.py:944
  170.0 3.4 %collective-permute-done.16.refs_2_ = bf16[3,72,384]{2,1,0:T(8,128)(2,1)S(1)} collective-permute-done((bf16[3,72,384]{2,1,0:T(8,128)(2,1)S(1)}, bf16[3,72,384]{2,1,0:T(8,128)(2,1)S(1)}, u32[]{:S(2)}, u32[]{:S(2)}) %collective-permute-start.16) | collective-permute-done | bytes 165920 | tf_op jit(solution)/shard_map/ppermute | solution.py:944
  174.1 3.8 %collective-permute-start.13 = (bf16[1,48,640]{2,1,0:T(8,128)(2,1)S(1)}, bf16[1,48,640]{2,1,0:T(8,128)(2,1)S(1)}, u32[]{:S(2)}, u32[]{:S(2)}) collective-permute-start(bf16[1,48,640]{2,1,0:T(8,128)(2,1)S(1)} %get-tuple-element.130), channel_id=1, source_target_pairs={{0,1},{1,2},{2,3},{3,0},{4,5},{5,6},{6,7},{7,4},{8,9},{9,10},{10,1... | collective-permute-start | bytes 184328 | tf_op jit(solution)/shard_map/ppermute | solution.py:1149
  180.2 3.4 %collective-permute-done.13.refs_2_ = bf16[1,48,640]{2,1,0:T(8,128)(2,1)S(1)} collective-permute-done((bf16[1,48,640]{2,1,0:T(8,128)(2,1)S(1)}, bf16[1,48,640]{2,1,0:T(8,128)(2,1)S(1)}, u32[]{:S(2)}, u32[]{:S(2)}) %collective-permute-start.13) | collective-permute-done | bytes 61472 | tf_op jit(solution)/shard_map/ppermute | solution.py:1149
  183.6 4.7 %collective-permute-done.14.refs_3_ = bf16[1,48,640]{2,1,0:T(8,128)(2,1)S(1)} collective-permute-done((bf16[1,48,640]{2,1,0:T(8,128)(2,1)S(1)}, bf16[1,48,640]{2,1,0:T(8,128)(2,1)S(1)}, u32[]{:S(2)}, u32[]{:S(2)}) %collective-permute-start.14) | collective-permute-done | bytes 61472 | tf_op jit(solution)/shard_map/ppermute | solution.py:1149
  194.0 6.4 %collective-permute-done.19.refs_4_ = bf16[1,48,640]{2,1,0:T(8,128)(2,1)S(1)} collective-permute-done((bf16[1,48,640]{2,1,0:T(8,128)(2,1)S(1)}, bf16[1,48,640]{2,1,0:T(8,128)(2,1)S(1)}, u32[]{:S(2)}, u32[]{:S(2)}) %collective-permute-start.19) | collective-permute-done | bytes 61472 | tf_op jit(solution)/shard_map/ppermute | solution.py:1149
  200.4 2.6 collective-permute-done.17.refs_2_
  204.2 3.5 %all-to-all-start.2 = ((bf16[4,576,256]{2,1,0:T(8,128)(2,1)}), bf16[4,576,256]{2,1,0:T(8,128)(2,1)S(1)}, u32[]{:S(2)}, u32[]{:S(2)}) async-start(bf16[4,576,256]{2,1,0:T(8,128)(2,1)} %get-tuple-element.140), calls=%async_computation.2 | async-start | bytes 2359296 | tf_op jit(solution)/shard_map/all_to_all | solution.py:1161
  213.1 5.5 %collective-permute-done.26.refs_4_ = bf16[2,3,72,384]{3,2,1,0:T(8,128)(2,1)S(1)} collective-permute-done((bf16[2,3,72,384]{3,2,1,0:T(8,128)(2,1)S(1)}, bf16[2,3,72,384]{3,2,1,0:T(8,128)(2,1)S(1)}, u32[]{:S(2)}, u32[]{:S(2)}) %collective-permute-start.26) | collective-permute-done | bytes 331808 | tf_op jit(solution)/shard_map/ppermute | solution.py:944
  218.6 6.6 %collective-permute-done.25.refs_2_ = bf16[2,3,72,384]{3,2,1,0:T(8,128)(2,1)S(1)} collective-permute-done((bf16[2,3,72,384]{3,2,1,0:T(8,128)(2,1)S(1)}, bf16[2,3,72,384]{3,2,1,0:T(8,128)(2,1)S(1)}, u32[]{:S(2)}, u32[]{:S(2)}) %collective-permute-start.25) | collective-permute-done | bytes 331808 | tf_op jit(solution)/shard_map/ppermute | solution.py:944
  225.9 2.5 join_line.1
  229.2 2.3 join_chips.1.refs_1_.refs_3_
  235.6 2.7 %join.2 = (f32[576,576]{1,0:T(8,128)}, f32[192,576]{1,0:T(8,128)}, f32[192,576]{1,0:T(8,128)}, f32[576,576]{1,0:T(8,128)}, f32[576,128]{1,0:T(8,128)S(1)}) custom-call(s32[4]{0:T(128)S(1)} %copy-done.20, bf16[4,4,1,48,640]{4,3,2,1,0:T(8,128)(2,1)S(1)} %copy-done.2, bf16[4,4,1,48,640]{4,3,2,1,0:T(8,128)(2,1)S(1)} %collective-permute-done.27.refs_2_, ...), custom_call_target="tpu_custom_call" | custom-call | flops 1000 | bytes 1000 | tf_op jit(solution)/shard_map/join/pallas_call | solution.py:376
  239.0 2.4 place.2.refs_5_
  241.4 7.5 %collective-permute-done.29.refs_4_ = bf16[2,2,3,72,384]{4,3,2,1,0:T(8,128)(2,1)S(1)} collective-permute-done((bf16[2,2,3,72,384]{4,3,2,1,0:T(8,128)(2,1)S(1)}, bf16[2,2,3,72,384]{4,3,2,1,0:T(8,128)(2,1)S(1)}, u32[]{:S(2)}, u32[]{:S(2)}) %collective-permute-start.29) | collective-permute-done | bytes 663584 | tf_op jit(solution)/shard_map/ppermute | solution.py:944
  250.8 3.4 %join_plane.1.refs_2_.refs_1_ = bf16[4,4,3,72,384]{4,3,2,1,0:T(8,128)(2,1)} custom-call(s32[4]{0:T(128)} %copy-done.17, bf16[2,2,3,72,384]{4,3,2,1,0:T(8,128)(2,1)} %get-tuple-element.138.refs_5_.refs_1_, bf16[2,2,3,72,384]{4,3,2,1,0:T(8,128)(2,1)} %collective-permute-done.28.refs_2_, bf16[2,2,3,72,384]{4,3,2,1,0:T(8,128)(2,1)} %get-tuple-element.141.refs_3_, ...), custom_call_target="tpu_custom_call" | custom-call | flops 1000 | bytes 1000 | tf_op jit(solution)/shard_map/join_plane/pallas_call | solution.py:376
  255.2 2.5 place.3.refs_3_
  260.8 6.1 %join.3 = (f32[2,4,72,1536]{3,2,1,0:T(8,128)}, f32[2,4,72,1536]{3,2,1,0:T(8,128)}, f32[2,4,72,1536]{3,2,1,0:T(8,128)}) custom-call(s32[4]{0:T(128)S(1)} %copy-done.21, bf16[4,4,3,72,384]{4,3,2,1,0:T(8,128)(2,1)S(1)} %copy-done, bf16[4,4,3,72,384]{4,3,2,1,0:T(8,128)(2,1)} %collective-permute-done.30.refs_2_, bf16[4,576,256]{2,1,0:T(8,128)(2,1)S(1)} %copy-done.4), custom_call_target="tpu_custom_call" | custom-call | flops 1000 | bytes 1000 | tf_op jit(solution)/shard_map/join/pallas_call | solution.py:376
  (169 shorter events, 61.8 us)
Async XLA Ops:
  0.7 43.9 %all-to-all-start = ((bf16[4,576,256]{2,1,0:T(8,128)(2,1)}), bf16[4,576,256]{2,1,0:T(8,128)(2,1)}, u32[]{:S(2)}, u32[]{:S(2)}) async-start(bf16[4,576,256]{2,1,0:T(8,128)(2,1)} %bitcast.39), calls=%async_computation | async-start | bytes 2359296 | tf_op jit(solution)/shard_map/all_to_all | solution.py:1161
  21.8 37.2 %collective-permute-start.1 = (bf16[576,256]{1,0:T(8,128)(2,1)S(1)}, bf16[576,256]{1,0:T(8,128)(2,1)S(1)}, u32[]{:S(2)}, u32[]{:S(2)}) collective-permute-start(bf16[576,256]{1,0:T(8,128)(2,1)S(1)} %get-tuple-element.88), channel_id=1, source_target_pairs={{0,2},{1,3},{2,0},{3,1},{4,6},{5,7},{6,4},{7,5},{8,10},{9,11},{10,... | collective-permute-start | bytes 884744 | tf_op jit(solution)/shard_map/ppermute | solution.py:1149
  24.7 34.2 %collective-permute-start.2 = (bf16[576,256]{1,0:T(8,128)(2,1)S(1)}, bf16[576,256]{1,0:T(8,128)(2,1)S(1)}, u32[]{:S(2)}, u32[]{:S(2)}) collective-permute-start(bf16[576,256]{1,0:T(8,128)(2,1)S(1)} %get-tuple-element.89), channel_id=1, source_target_pairs={{0,3},{1,0},{2,1},{3,2},{4,7},{5,4},{6,5},{7,6},{8,11},{9,8},{10,9... | collective-permute-start | bytes 884744 | tf_op jit(solution)/shard_map/ppermute | solution.py:1149
  26.2 32.8 %collective-permute-start = (bf16[576,256]{1,0:T(8,128)(2,1)S(1)}, bf16[576,256]{1,0:T(8,128)(2,1)S(1)}, u32[]{:S(2)}, u32[]{:S(2)}) collective-permute-start(bf16[576,256]{1,0:T(8,128)(2,1)S(1)} %get-tuple-element.86.refs_6_), channel_id=1, source_target_pairs={{0,1},{1,2},{2,3},{3,0},{4,5},{5,6},{6,7},{7,4},{8,9},{9,10},{10,1... | collective-permute-start | bytes 884744 | tf_op jit(solution)/shard_map/ppermute | solution.py:1149
  96.3 8.0 %collective-permute-start.3 = (bf16[4,4,3,72,384]{4,3,2,1,0:T(8,128)(2,1)}, bf16[4,4,3,72,384]{4,3,2,1,0:T(8,128)(2,1)}, u32[]{:S(2)}, u32[]{:S(2)}) collective-permute-start(bf16[4,4,3,72,384]{4,3,2,1,0:T(8,128)(2,1)} %get-tuple-element.108), channel_id=1, source_target_pairs={{0,4},{4,0},{8,12},{12,8},{16,20},{20,16},{24,28},{28,24},{1,5},{5... | collective-permute-start | bytes 7962632 | tf_op jit(solution)/shard_map/ppermute | solution.py:944
  96.3 51.0 %all-to-all-start.1 = ((bf16[4,576,256]{2,1,0:T(8,128)(2,1)}), bf16[4,576,256]{2,1,0:T(8,128)(2,1)S(1)}, u32[]{:S(2)}, u32[]{:S(2)}) async-start(bf16[4,576,256]{2,1,0:T(8,128)(2,1)} %get-tuple-element.97), calls=%async_computation.1 | async-start | bytes 2359296 | tf_op jit(solution)/shard_map/all_to_all | solution.py:1161
  109.0 26.9 %collective-permute-start.5 = (bf16[2,2,3,72,384]{4,3,2,1,0:T(8,128)(2,1)}, bf16[2,2,3,72,384]{4,3,2,1,0:T(8,128)(2,1)S(1)}, u32[]{:S(2)}, u32[]{:S(2)}) collective-permute-start(bf16[2,2,3,72,384]{4,3,2,1,0:T(8,128)(2,1)} %get-tuple-element.114), channel_id=1, source_target_pairs={{0,16},{4,20},{8,24},{12,28},{16,0},{20,4},{24,8},{28,12},{1,17},{... | collective-permute-start | bytes 1990664 | tf_op jit(solution)/shard_map/ppermute | solution.py:944
  110.5 25.4 %collective-permute-start.4 = (bf16[2,2,3,72,384]{4,3,2,1,0:T(8,128)(2,1)}, bf16[2,2,3,72,384]{4,3,2,1,0:T(8,128)(2,1)S(1)}, u32[]{:S(2)}, u32[]{:S(2)}) collective-permute-start(bf16[2,2,3,72,384]{4,3,2,1,0:T(8,128)(2,1)} %get-tuple-element.109.refs_17_), channel_id=1, source_target_pairs={{0,8},{4,12},{8,0},{12,4},{16,24},{20,28},{24,16},{28,20},{1,9},{5... | collective-permute-start | bytes 1990664 | tf_op jit(solution)/shard_map/ppermute | solution.py:944
  140.7 10.5 %collective-permute-start.11 = (bf16[2,3,72,384]{3,2,1,0:T(8,128)(2,1)}, bf16[2,3,72,384]{3,2,1,0:T(8,128)(2,1)}, u32[]{:S(2)}, u32[]{:S(2)}) collective-permute-start(bf16[2,3,72,384]{3,2,1,0:T(8,128)(2,1)} %get-tuple-element.125), channel_id=1, source_target_pairs={{0,8},{4,12},{8,0},{12,4},{16,24},{20,28},{24,16},{28,20},{1,9},{5... | collective-permute-start | bytes 995336 | tf_op jit(solution)/shard_map/ppermute | solution.py:944
  141.3 10.2 %collective-permute-start.10 = (bf16[2,3,72,384]{3,2,1,0:T(8,128)(2,1)}, bf16[2,3,72,384]{3,2,1,0:T(8,128)(2,1)}, u32[]{:S(2)}, u32[]{:S(2)}) collective-permute-start(bf16[2,3,72,384]{3,2,1,0:T(8,128)(2,1)} %get-tuple-element.118.refs_3_), channel_id=1, source_target_pairs={{0,16},{4,20},{8,24},{12,28},{16,0},{20,4},{24,8},{28,12},{1,17},{... | collective-permute-start | bytes 995336 | tf_op jit(solution)/shard_map/ppermute | solution.py:944
  153.9 9.5 %collective-permute-start.12 = (bf16[2,3,72,384]{3,2,1,0:T(8,128)(2,1)S(1)}, bf16[2,3,72,384]{3,2,1,0:T(8,128)(2,1)S(1)}, u32[]{:S(2)}, u32[]{:S(2)}) collective-permute-start(bf16[2,3,72,384]{3,2,1,0:T(8,128)(2,1)S(1)} %get-tuple-element.127.refs_3_), channel_id=1, source_target_pairs={{0,1},{1,0},{2,3},{3,2},{4,5},{5,4},{6,7},{7,6},{8,9},{9,8},{10,11... | collective-permute-start | bytes 995336 | tf_op jit(solution)/shard_map/ppermute | solution.py:944
  155.9 10.7 %collective-permute-start.7 = (bf16[4,1,48,640]{3,2,1,0:T(8,128)(2,1)S(1)}, bf16[4,1,48,640]{3,2,1,0:T(8,128)(2,1)S(1)}, u32[]{:S(2)}, u32[]{:S(2)}) collective-permute-start(bf16[4,1,48,640]{3,2,1,0:T(8,128)(2,1)S(1)} %copy-done.27), channel_id=1, source_target_pairs={{0,8},{4,12},{8,0},{12,4},{16,24},{20,28},{24,16},{28,20},{1,9},{5... | collective-permute-start | bytes 737288 | tf_op jit(solution)/shard_map/ppermute | solution.py:944
  157.5 11.9 %collective-permute-start.8 = (bf16[4,1,48,640]{3,2,1,0:T(8,128)(2,1)S(1)}, bf16[4,1,48,640]{3,2,1,0:T(8,128)(2,1)S(1)}, u32[]{:S(2)}, u32[]{:S(2)}) collective-permute-start(bf16[4,1,48,640]{3,2,1,0:T(8,128)(2,1)S(1)} %copy-done.25), channel_id=1, source_target_pairs={{0,16},{4,20},{8,24},{12,28},{16,0},{20,4},{24,8},{28,12},{1,17},{... | collective-permute-start | bytes 737288 | tf_op jit(solution)/shard_map/ppermute | solution.py:944
  157.9 11.4 %collective-permute-start.9 = (bf16[4,1,48,640]{3,2,1,0:T(8,128)(2,1)S(1)}, bf16[4,1,48,640]{3,2,1,0:T(8,128)(2,1)S(1)}, u32[]{:S(2)}, u32[]{:S(2)}) collective-permute-start(bf16[4,1,48,640]{3,2,1,0:T(8,128)(2,1)S(1)} %copy-done.23), channel_id=1, source_target_pairs={{0,24},{4,28},{8,16},{12,20},{16,8},{20,12},{24,0},{28,4},{1,25},{... | collective-permute-start | bytes 737288 | tf_op jit(solution)/shard_map/ppermute | solution.py:944
  164.0 9.5 %collective-permute-start.16 = (bf16[3,72,384]{2,1,0:T(8,128)(2,1)S(1)}, bf16[3,72,384]{2,1,0:T(8,128)(2,1)S(1)}, u32[]{:S(2)}, u32[]{:S(2)}) collective-permute-start(bf16[3,72,384]{2,1,0:T(8,128)(2,1)S(1)} %get-tuple-element.128.refs_5_), channel_id=1, source_target_pairs={{0,2},{1,3},{2,0},{3,1},{4,6},{5,7},{6,4},{7,5},{8,10},{9,11},{10,... | collective-permute-start | bytes 497672 | tf_op jit(solution)/shard_map/ppermute | solution.py:944
  174.0 14.9 %collective-permute-start.20 = (bf16[3,72,384]{2,1,0:T(8,128)(2,1)S(1)}, bf16[3,72,384]{2,1,0:T(8,128)(2,1)S(1)}, u32[]{:S(2)}, u32[]{:S(2)}) collective-permute-start(bf16[3,72,384]{2,1,0:T(8,128)(2,1)S(1)} %total.1.refs_5_.refs_1_), channel_id=1, source_target_pairs={{0,2},{1,3},{2,0},{3,1},{4,6},{5,7},{6,4},{7,5},{8,10},{9,11},{10,... | collective-permute-start | bytes 497672 | tf_op jit(solution)/shard_map/ppermute | solution.py:944
  174.1 9.6 %collective-permute-start.13 = (bf16[1,48,640]{2,1,0:T(8,128)(2,1)S(1)}, bf16[1,48,640]{2,1,0:T(8,128)(2,1)S(1)}, u32[]{:S(2)}, u32[]{:S(2)}) collective-permute-start(bf16[1,48,640]{2,1,0:T(8,128)(2,1)S(1)} %get-tuple-element.130), channel_id=1, source_target_pairs={{0,1},{1,2},{2,3},{3,0},{4,5},{5,6},{6,7},{7,4},{8,9},{9,10},{10,1... | collective-permute-start | bytes 184328 | tf_op jit(solution)/shard_map/ppermute | solution.py:1149
  177.9 10.5 %collective-permute-start.14 = (bf16[1,48,640]{2,1,0:T(8,128)(2,1)S(1)}, bf16[1,48,640]{2,1,0:T(8,128)(2,1)S(1)}, u32[]{:S(2)}, u32[]{:S(2)}) collective-permute-start(bf16[1,48,640]{2,1,0:T(8,128)(2,1)S(1)} %get-tuple-element.131), channel_id=1, source_target_pairs={{0,2},{1,3},{2,0},{3,1},{4,6},{5,7},{6,4},{7,5},{8,10},{9,11},{10,... | collective-permute-start | bytes 184328 | tf_op jit(solution)/shard_map/ppermute | solution.py:1149
  177.9 10.4 %collective-permute-start.15 = (bf16[1,48,640]{2,1,0:T(8,128)(2,1)S(1)}, bf16[1,48,640]{2,1,0:T(8,128)(2,1)S(1)}, u32[]{:S(2)}, u32[]{:S(2)}) collective-permute-start(bf16[1,48,640]{2,1,0:T(8,128)(2,1)S(1)} %get-tuple-element.132), channel_id=1, source_target_pairs={{0,3},{1,0},{2,1},{3,2},{4,7},{5,4},{6,5},{7,6},{8,11},{9,8},{10,9... | collective-permute-start | bytes 184328 | tf_op jit(solution)/shard_map/ppermute | solution.py:1149
  189.5 14.0 %collective-permute-start.24 = (bf16[2,3,72,384]{3,2,1,0:T(8,128)(2,1)S(1)}, bf16[2,3,72,384]{3,2,1,0:T(8,128)(2,1)S(1)}, u32[]{:S(2)}, u32[]{:S(2)}) collective-permute-start(bf16[2,3,72,384]{3,2,1,0:T(8,128)(2,1)S(1)} %join_far.1.refs_5_.refs_1_), channel_id=1, source_target_pairs={{0,1},{1,0},{2,3},{3,2},{4,5},{5,4},{6,7},{7,6},{8,9},{9,8},{10,11... | collective-permute-start | bytes 995336 | tf_op jit(solution)/shard_map/ppermute | solution.py:944
  190.8 9.6 %collective-permute-start.19 = (bf16[1,48,640]{2,1,0:T(8,128)(2,1)S(1)}, bf16[1,48,640]{2,1,0:T(8,128)(2,1)S(1)}, u32[]{:S(2)}, u32[]{:S(2)}) collective-permute-start(bf16[1,48,640]{2,1,0:T(8,128)(2,1)S(1)} %add_seq.1.refs_3_.refs_1_), channel_id=1, source_target_pairs={{0,3},{1,0},{2,1},{3,2},{4,7},{5,4},{6,5},{7,6},{8,11},{9,8},{10,9... | collective-permute-start | bytes 184328 | tf_op jit(solution)/shard_map/ppermute | solution.py:1149
  191.5 8.9 %collective-permute-start.18 = (bf16[1,48,640]{2,1,0:T(8,128)(2,1)S(1)}, bf16[1,48,640]{2,1,0:T(8,128)(2,1)S(1)}, u32[]{:S(2)}, u32[]{:S(2)}) collective-permute-start(bf16[1,48,640]{2,1,0:T(8,128)(2,1)S(1)} %add_seq.1.refs_3_.refs_1_), channel_id=1, source_target_pairs={{0,2},{1,3},{2,0},{3,1},{4,6},{5,7},{6,4},{7,5},{8,10},{9,11},{10,... | collective-permute-start | bytes 184328 | tf_op jit(solution)/shard_map/ppermute | solution.py:1149
  193.1 9.9 %collective-permute-start.17 = (bf16[1,48,640]{2,1,0:T(8,128)(2,1)S(1)}, bf16[1,48,640]{2,1,0:T(8,128)(2,1)S(1)}, u32[]{:S(2)}, u32[]{:S(2)}) collective-permute-start(bf16[1,48,640]{2,1,0:T(8,128)(2,1)S(1)} %add_seq.1.refs_3_.refs_1_), channel_id=1, source_target_pairs={{0,1},{1,2},{2,3},{3,0},{4,5},{5,6},{6,7},{7,4},{8,9},{9,10},{10,1... | collective-permute-start | bytes 184328 | tf_op jit(solution)/shard_map/ppermute | solution.py:1149
  204.2 45.0 %all-to-all-start.2 = ((bf16[4,576,256]{2,1,0:T(8,128)(2,1)}), bf16[4,576,256]{2,1,0:T(8,128)(2,1)S(1)}, u32[]{:S(2)}, u32[]{:S(2)}) async-start(bf16[4,576,256]{2,1,0:T(8,128)(2,1)} %get-tuple-element.140), calls=%async_computation.2 | async-start | bytes 2359296 | tf_op jit(solution)/shard_map/all_to_all | solution.py:1161
  207.8 10.8 %collective-permute-start.26 = (bf16[2,3,72,384]{3,2,1,0:T(8,128)(2,1)S(1)}, bf16[2,3,72,384]{3,2,1,0:T(8,128)(2,1)S(1)}, u32[]{:S(2)}, u32[]{:S(2)}) collective-permute-start(bf16[2,3,72,384]{3,2,1,0:T(8,128)(2,1)S(1)} %get-tuple-element.135.refs_3_), channel_id=1, source_target_pairs={{0,8},{4,12},{8,0},{12,4},{16,24},{20,28},{24,16},{28,20},{1,9},{5... | collective-permute-start | bytes 995336 | tf_op jit(solution)/shard_map/ppermute | solution.py:944
  209.2 16.0 %collective-permute-start.25 = (bf16[2,3,72,384]{3,2,1,0:T(8,128)(2,1)S(1)}, bf16[2,3,72,384]{3,2,1,0:T(8,128)(2,1)S(1)}, u32[]{:S(2)}, u32[]{:S(2)}) collective-permute-start(bf16[2,3,72,384]{3,2,1,0:T(8,128)(2,1)S(1)} %get-tuple-element.137.refs_1_.refs_5_), channel_id=1, source_target_pairs={{0,16},{4,20},{8,24},{12,28},{16,0},{20,4},{24,8},{28,12},{1,17},{... | collective-permute-start | bytes 995336 | tf_op jit(solution)/shard_map/ppermute | solution.py:944
  209.6 18.8 %collective-permute-start.23 = (bf16[4,1,48,640]{3,2,1,0:T(8,128)(2,1)S(1)}, bf16[4,1,48,640]{3,2,1,0:T(8,128)(2,1)S(1)}, u32[]{:S(2)}, u32[]{:S(2)}) collective-permute-start(bf16[4,1,48,640]{3,2,1,0:T(8,128)(2,1)S(1)} %join_seq.1.refs_3_.refs_1_), channel_id=1, source_target_pairs={{0,24},{4,28},{8,16},{12,20},{16,8},{20,12},{24,0},{28,4},{1,25},{... | collective-permute-start | bytes 737288 | tf_op jit(solution)/shard_map/ppermute | solution.py:944
  211.3 17.1 %collective-permute-start.22 = (bf16[4,1,48,640]{3,2,1,0:T(8,128)(2,1)S(1)}, bf16[4,1,48,640]{3,2,1,0:T(8,128)(2,1)S(1)}, u32[]{:S(2)}, u32[]{:S(2)}) collective-permute-start(bf16[4,1,48,640]{3,2,1,0:T(8,128)(2,1)S(1)} %join_seq.1.refs_3_.refs_1_), channel_id=1, source_target_pairs={{0,16},{4,20},{8,24},{12,28},{16,0},{20,4},{24,8},{28,12},{1,17},{... | collective-permute-start | bytes 737288 | tf_op jit(solution)/shard_map/ppermute | solution.py:944
  211.8 16.6 %collective-permute-start.21 = (bf16[4,1,48,640]{3,2,1,0:T(8,128)(2,1)S(1)}, bf16[4,1,48,640]{3,2,1,0:T(8,128)(2,1)S(1)}, u32[]{:S(2)}, u32[]{:S(2)}) collective-permute-start(bf16[4,1,48,640]{3,2,1,0:T(8,128)(2,1)S(1)} %join_seq.1.refs_3_.refs_1_), channel_id=1, source_target_pairs={{0,8},{4,12},{8,0},{12,4},{16,24},{20,28},{24,16},{28,20},{1,9},{5... | collective-permute-start | bytes 737288 | tf_op jit(solution)/shard_map/ppermute | solution.py:944
  231.6 17.3 %collective-permute-start.29 = (bf16[2,2,3,72,384]{4,3,2,1,0:T(8,128)(2,1)S(1)}, bf16[2,2,3,72,384]{4,3,2,1,0:T(8,128)(2,1)S(1)}, u32[]{:S(2)}, u32[]{:S(2)}) collective-permute-start(bf16[2,2,3,72,384]{4,3,2,1,0:T(8,128)(2,1)S(1)} %copy-done.36), channel_id=1, source_target_pairs={{0,16},{4,20},{8,24},{12,28},{16,0},{20,4},{24,8},{28,12},{1,17},{... | collective-permute-start | bytes 1990664 | tf_op jit(solution)/shard_map/ppermute | solution.py:944
  232.1 17.1 %collective-permute-start.28 = (bf16[2,2,3,72,384]{4,3,2,1,0:T(8,128)(2,1)S(1)}, bf16[2,2,3,72,384]{4,3,2,1,0:T(8,128)(2,1)}, u32[]{:S(2)}, u32[]{:S(2)}) collective-permute-start(bf16[2,2,3,72,384]{4,3,2,1,0:T(8,128)(2,1)S(1)} %copy-done.32), channel_id=1, source_target_pairs={{0,8},{4,12},{8,0},{12,4},{16,24},{20,28},{24,16},{28,20},{1,9},{5... | collective-permute-start | bytes 1990664 | tf_op jit(solution)/shard_map/ppermute | solution.py:944
  254.2 5.3 %collective-permute-start.30 = (bf16[4,4,3,72,384]{4,3,2,1,0:T(8,128)(2,1)}, bf16[4,4,3,72,384]{4,3,2,1,0:T(8,128)(2,1)}, u32[]{:S(2)}, u32[]{:S(2)}) collective-permute-start(bf16[4,4,3,72,384]{4,3,2,1,0:T(8,128)(2,1)} %join_plane.1.refs_2_.refs_1_), channel_id=1, source_target_pairs={{0,4},{4,0},{8,12},{12,8},{16,20},{20,16},{24,28},{28,24},{1,5},{5... | collective-permute-start | bytes 7962632 | tf_op jit(solution)/shard_map/ppermute | solution.py:944
  (50 other events, 238.0 us)
where the time goes:
time: 268 us; the launch traced here: 267 us
  Pallas kernels  111 us (41%)
  waiting for transfers between devices  70.2 us (26%)
  starting transfers between devices  52.5 us (20%)
  local copies, waits for them, and re-layouts  29.7 us (11%)
    pallas_call x22, Pallas kernels, run(): pl.pallas_call(body, grid=grid, in_specs=[SMEM] + (in_specs or [FULL] * t...  111 us
    ppermute x22, waiting for transfers between devices, swap(): return lax.ppermute(values, axis, [(k, k ^ bits) for k in range(count)])  39.2 us
    unnamed x99, local copies, waits for them, and re-layouts  21 us
    ppermute x22, starting transfers between devices, swap(): return lax.ppermute(values, axis, [(k, k ^ bits) for k in range(count)])  20 us
    all_to_all x3, starting transfers between devices, exchange(): return lax.all_to_all(values, 'seq', 0, 0)  18 us
    ppermute x9, waiting for transfers between devices, shift(): return lax.ppermute(values, 'seq', [(k, (k + step) % 4) for k in range(4)])  17.1 us
    ppermute x9, starting transfers between devices, shift(): return lax.ppermute(values, 'seq', [(k, (k + step) % 4) for k in range(4)])  14.4 us
    all_to_all x3, waiting for transfers between devices, exchange(): return lax.all_to_all(values, 'seq', 0, 0)  13.9 us
  transfers between devices with their start and end apart: 34, of which 17 were waited for; matrix products, arithmetic and copies ran while one was open for 7% of the time, Pallas kernels for 24%

commit v1 on v0

--- a/solution.py
+++ b/solution.py
@@ -928,17 +928,6 @@
         outs[k][1 - mine] = ins[2 * k + 1][...]
 
 
-def join_plane_kernel(routes, info, *refs):
-    ins, out_ref = refs[:-1], refs[-1]
-    for k, (first, places) in enumerate(routes):
-        mine = bit_of(info[2], first)
-        own_ref, in_ref = ins[2 * k : 2 * k + 2]
-        for t in range(2):
-            for at, z in enumerate(places):
-                out_ref[plane_at(first, mine, t), z] = own_ref[t, at]
-                out_ref[plane_at(first, 1 - mine, t), z] = in_ref[t, at]
-
-
 def swap(values, axis, bits):
     count = 8 if axis == "dp" else 4
     return lax.ppermute(values, axis, [(k, k ^ bits) for k in range(count)])
@@ -993,18 +982,12 @@
                 join_near_kernel, [self.outs, self.next], [shape_of((places, *piece))] * count
             )
             self.next = [swap(self.outs[k], "dp", line[k]) for k in range(count)]
-        elif self.stage in (7, 8):
+        elif self.stage == 7:
             operands = []
             for k in range(count):
                 operands += [self.outs[k], self.next[k]]
-            if self.stage == 7:
-                self.outs = self.call(
-                    join_line_kernel, operands, [shape_of((2, places, *piece))] * count
-                )
-                self.next = [swap(self.outs[k], "dp", plane[k]) for k in range(count)]
-            else:
-                self.outs = self.call(join_plane_kernel, operands, shape_of((4, 4, *piece)))
-                self.next = swap(self.outs, "dp", 1)
+            self.outs = self.call(join_line_kernel, operands, [shape_of((2, places, *piece))] * count)
+            self.next = [swap(self.outs[k], "dp", plane[k]) for k in range(count)]
         self.stage += 1
 
 
@@ -1074,30 +1057,43 @@
         self.stage += 1
 
 
-def join_wide_kernel(info, own_ref, in_ref, *out_refs):
-    _, parts, count, rows, cols = own_ref.shape
-    for ref, core in ((own_ref, info[1]), (in_ref, 1 - info[1])):
-        for z in range(parts):
-            for k in range(count):
-                out_refs[k][core, 0, :, z * cols : (z + 1) * cols] = wide(ref[0, z, k])
-
-
-def join_wide(info, own, came):
-    _, parts, count, rows, cols = own.shape
-    piece = pl.BlockSpec((1, parts, count, rows, cols), lambda p: (p, 0, 0, 0, 0))
+def join_wide_kernel(routes, info, *refs):
+    parts, outs, refs = refs[:8], refs[8:11], refs[11:]
+    buffers, sems = refs[:3], refs[3]
+    _, _, count, rows, cols = parts[0].shape
+    copies = [pltpu.make_async_copy(buffers[w], outs[w], sems.at[w]) for w in range(count)]
+    for w in range(count):
+        for side in range(4):
+            core = info[1] if side < 2 else 1 - info[1]
+            for k, (first, places) in enumerate(routes):
+                mine = bit_of(info[2], first)
+                mine = mine if side % 2 == 0 else 1 - mine
+                ref = parts[2 * side + k]
+                for t in range(2):
+                    p = plane_at(first, mine, t)
+                    for at, z in enumerate(places):
+                        buffers[w][core, p, :, z * cols : (z + 1) * cols] = wide(ref[t, at, w])
+        copies[w].start()
+    for copy in copies:
+        copy.wait()
+
+
+def join_wide(info, routes, parts):
+    _, _, count, rows, cols = parts[0].shape
+    shape = (2, 4, rows, 4 * cols)
     outs = run(
-        join_wide_kernel,
+        partial(join_wide_kernel, routes),
         "join",
         info,
-        [own, came],
-        [shape_of((2, 4, rows, parts * cols), jnp.float32)] * count,
-        [],
-        16,
-        (4,),
-        [piece] * 2,
-        [pl.BlockSpec((2, 1, rows, parts * cols), lambda p: (0, p, 0, 0))] * count,
-    )
-    return [v.reshape(8 * rows, parts * cols) for v in outs]
+        parts,
+        [shape_of(shape, jnp.float32)] * count,
+        [pltpu.VMEM(shape, jnp.float32)] * count + [pltpu.SemaphoreType.DMA((3,))],
+        60,
+        (1,),
+        [once(*v.shape) for v in parts],
+        [ANY] * count,
+    )
+    return [v.reshape(8 * rows, 4 * cols) for v in outs]
 
 
 def join_attn_kernel(
@@ -1250,6 +1246,7 @@
     tokens_out = exchange(tokens_grad)
     Order.windows = True
     wide_sum.step()
+    near_came = [swap(part, "dp", 1) for part in wide_sum.outs]
     attn_sum.step()
     square = shape_of((model_width, model_width), jnp.float32)
     narrow = shape_of((kv_width, model_width), jnp.float32)
@@ -1266,11 +1263,14 @@
         [once(*attn_sum.outs.shape)] * 2,
         [once(*v.shape) for v in shapes],
     )
+    Order.also = tuple(near_came)
     mixed_out = place(info, mixed_out)
+    far_came = [swap(part, "dp", 1) for part in wide_sum.next]
     Order.also = (tokens_out,)
-    wide_sum.step()
     tokens_out = place(info, tokens_out)
-    w_gate_sum, w_up_sum, w_down_sum = join_wide(info, wide_sum.outs, wide_sum.next)
+    w_gate_sum, w_up_sum, w_down_sum = join_wide(
+        info, TWO_ROUTES, [*wide_sum.outs, *wide_sum.next, *near_came, *far_came]
+    )
     return (
         jnp.swapaxes(mixed_out, 1, 2),
         jnp.swapaxes(tokens_out, 1, 2),

time: 268 us -> 264 us (0.985)
    pallas_call x22 -> x21, Pallas kernels: 111 us -> 109 us  [run(): pl.pallas_call(body, grid=grid, in_specs=[SMEM] + (in_specs or [FULL] * t...]
    ppermute x22 -> x25, waiting for transfers between devices: 39.2 us -> 37.6 us  [swap(): return lax.ppermute(values, axis, [(k, k ^ bits) for k in range(count)])]
    ppermute x22 -> x25, starting transfers between devices: 20 us -> 21.2 us  [swap(): return lax.ppermute(values, axis, [(k, k ^ bits) for k in range(count)])]
    unnamed x99 -> x89, local copies, waits for them, and re-layouts: 21 us -> 20.2 us
  transfers between devices with their start and end apart: 34 -> 37, of which waited for: 17 -> 15; matrix products, arithmetic and copies ran while one was open for 7% -> 7% of each run, Pallas kernels for 24% -> 24%
where the time goes in v1:
time: 264 us; the launch traced here: 263 us
  Pallas kernels  109 us (41%)
  waiting for transfers between devices  67.9 us (26%)
  starting transfers between devices  53.6 us (20%)
  local copies, waits for them, and re-layouts  28.9 us (11%)
    pallas_call x21, Pallas kernels, run(): pl.pallas_call(body, grid=grid, in_specs=[SMEM] + (in_specs or [FULL] * t...  109 us
    ppermute x25, waiting for transfers between devices, swap(): return lax.ppermute(values, axis, [(k, k ^ bits) for k in range(count)])  37.6 us
    ppermute x25, starting transfers between devices, swap(): return lax.ppermute(values, axis, [(k, k ^ bits) for k in range(count)])  21.2 us
    unnamed x89, local copies, waits for them, and re-layouts  20.2 us
    all_to_all x3, starting transfers between devices, exchange(): return lax.all_to_all(values, 'seq', 0, 0)  18 us
    ppermute x9, waiting for transfers between devices, shift(): return lax.ppermute(values, 'seq', [(k, (k + step) % 4) for k in range(4)])  17.1 us
    ppermute x9, starting transfers between devices, shift(): return lax.ppermute(values, 'seq', [(k, (k + step) % 4) for k in range(4)])  14.4 us
    all_to_all x3, waiting for transfers between devices, exchange(): return lax.all_to_all(values, 'seq', 0, 0)  13.2 us
  transfers between devices with their start and end apart: 37, of which 15 were waited for; matrix products, arithmetic and copies ran while one was open for 7% of the time, Pallas kernels for 24%

profile of v1, /device:TPU:0, one launch (start us, length us, event | category | flops | bytes accessed | tf_op | source)
XLA Modules:
  0.0 262.7 jit_solution(16412120407312025795)
XLA Ops:
  0.7 6.5 %all-to-all-start = ((bf16[4,576,256]{2,1,0:T(8,128)(2,1)}), bf16[4,576,256]{2,1,0:T(8,128)(2,1)}, u32[]{:S(2)}, u32[]{:S(2)}) async-start(bf16[4,576,256]{2,1,0:T(8,128)(2,1)} %bitcast.39), calls=%async_computation | async-start | bytes 2359296 | tf_op jit(solution)/shard_map/all_to_all | solution.py:1157
  14.1 4.0 %copy.33 = bf16[576,1536]{0,1:T(8,128)(2,1)} copy(bf16[576,1536]{1,0:T(8,128)(2,1)} %refs_14_.1) | data formatting | bytes 3538944 | tf_op args[7]
  22.5 3.0 %collective-permute-start.1 = (bf16[576,256]{1,0:T(8,128)(2,1)S(1)}, bf16[576,256]{1,0:T(8,128)(2,1)S(1)}, u32[]{:S(2)}, u32[]{:S(2)}) collective-permute-start(bf16[576,256]{1,0:T(8,128)(2,1)S(1)} %get-tuple-element.88), channel_id=1, source_target_pairs={{0,2},{1,3},{2,0},{3,1},{4,6},{5,7},{6,4},{7,5},{8,10},{9,11},{10,... | collective-permute-start | bytes 884744 | tf_op jit(solution)/shard_map/ppermute | solution.py:1145
  27.5 3.9 %copy.34.refs_12_ = bf16[1536,576]{1,0:T(8,128)(2,1)} copy(bf16[1536,576]{0,1:T(8,128)(2,1)} %param.20) | data formatting | bytes 3538944 | tf_op jit(solution)/shard_map/optimization_barrier | solution.py:1199
  31.4 13.2 %all-to-all-done.refs_1_.refs_11_ = bf16[4,576,256]{2,1,0:T(8,128)(2,1)} async-done(((bf16[4,576,256]{2,1,0:T(8,128)(2,1)}), bf16[4,576,256]{2,1,0:T(8,128)(2,1)}, u32[]{:S(2)}, u32[]{:S(2)}) %all-to-all-start) | async-done | bytes 1179680 | tf_op jit(solution)/shard_map/all_to_all | solution.py:1157
  44.6 14.4 %attend.1 = (bf16[4,576,256]{2,1,0:T(8,128)(2,1)}, bf16[3,4,192,256]{3,2,1,0:T(8,128)(2,1)}, bf16[3,4,64,256]{3,2,1,0:T(8,128)(2,1)}, bf16[3,4,64,256]{3,2,1,0:T...) custom-call(s32[4]{0:T(128)} %copy-done.15, ...), custom_call_target="tpu_custom_call" | custom-call | flops 1000 | bytes 1000 | tf_op jit(solution)/shard_map/attend/pallas_call | solution.py:376
  59.8 35.7 %ffn.1 = (bf16[4,576,256]{2,1,0:T(8,128)(2,1)}, f32[4,576,256]{2,1,0:T(8,128)}, bf16[4,576,256]{2,1,0:T(8,128)(2,1)}, bf16[4,576,256]{2,1,0:T(8,128)(2,1)}, f32[...) custom-call(s32[4]{0:T(128)S(1)} %copy-done.16, ...), custom_call_target="tpu_custom_call" | custom-call | flops 1000 | bytes 1000 | tf_op jit(solution)/shard_map/ffn/pallas_call | solution.py:376
  96.3 8.0 %all-to-all-start.1 = ((bf16[4,576,256]{2,1,0:T(8,128)(2,1)}), bf16[4,576,256]{2,1,0:T(8,128)(2,1)S(1)}, u32[]{:S(2)}, u32[]{:S(2)}) async-start(bf16[4,576,256]{2,1,0:T(8,128)(2,1)} %get-tuple-element.97), calls=%async_computation.1 | async-start | bytes 2359296 | tf_op jit(solution)/shard_map/all_to_all | solution.py:1157
  104.4 4.6 %split_plane.1 = (bf16[2,2,3,72,384]{4,3,2,1,0:T(8,128)(2,1)}, f32[2,2,3,72,384]{4,3,2,1,0:T(8,128)}, bf16[2,2,3,72,384]{4,3,2,1,0:T(8,128)(2,1)}, f32[2,2,3,72,384]{4,3,2,1,0:T(8,128)}) custom-call(s32[4]{0:T(128)} %copy-done.15, bf16[4,4,3,72,384]{4,3,2,1,0:T(8,128)(2,1)} %get-tuple-element.107.refs_1_, ...), custom_call_target="tpu_custom_call" | custom-call | flops 1000 | bytes 1000 | tf_op jit(solution)/shard_map/split_plane/pallas_call | solution.py:376
  112.0 23.9 %back.1 = (bf16[4,576,256]{2,1,0:T(8,128)(2,1)}, bf16[4,4,1,48,640]{4,3,2,1,0:T(8,128)(2,1)}, bf16[4,4,1,48,640]{4,3,2,1,0:T(8,128)(2,1)}) custom-call(s32[4]{0:T(128)} %copy-done.15, bf16[3,4,192,256]{3,2,1,0:T(8,128)(2,1)} %get-tuple-element.98.refs_1_, bf16[3,4,64,256]{3,2,1,0:T(8,128)(2,1)} %get-tuple-element.99.refs_2_, ...), custom_call_target="tpu_custom_call" | custom-call | flops 1000 | bytes 1000 | tf_op jit(solution)/shard_map/back/pallas_call | solution.py:376
  137.0 3.7 %split_line.1 = (bf16[2,3,72,384]{3,2,1,0:T(8,128)(2,1)}, f32[2,3,72,384]{3,2,1,0:T(8,128)}, bf16[2,3,72,384]{3,2,1,0:T(8,128)(2,1)}, f32[2,3,72,384]{3,2,1,0:T(8,128)}) custom-call(s32[4]{0:T(128)} %copy-done.15, f32[2,2,3,72,384]{4,3,2,1,0:T(8,128)} %get-tuple-element.112.refs_1_, bf16[2,2,3,72,384]{4,3,2,1,0:T(8,128)(2,1)} %copy-done.34, ...), custom_call_target="tpu_custom_call" | custom-call | flops 1000 | bytes 1000 | tf_op jit(solution)/shard_map/split_line/pallas_call | solution.py:376
  147.3 3.9 %collective-permute-done.11.refs_4_ = bf16[2,3,72,384]{3,2,1,0:T(8,128)(2,1)} collective-permute-done((bf16[2,3,72,384]{3,2,1,0:T(8,128)(2,1)}, bf16[2,3,72,384]{3,2,1,0:T(8,128)(2,1)}, u32[]{:S(2)}, u32[]{:S(2)}) %collective-permute-start.11) | collective-permute-done | bytes 331808 | tf_op jit(solution)/shard_map/ppermute | solution.py:933
  159.5 3.9 %collective-permute-done.12.refs_2_ = bf16[2,3,72,384]{3,2,1,0:T(8,128)(2,1)S(1)} collective-permute-done((bf16[2,3,72,384]{3,2,1,0:T(8,128)(2,1)S(1)}, bf16[2,3,72,384]{3,2,1,0:T(8,128)(2,1)S(1)}, u32[]{:S(2)}, u32[]{:S(2)}) %collective-permute-start.12) | collective-permute-done | bytes 331808 | tf_op jit(solution)/shard_map/ppermute | solution.py:933
  163.9 2.7 %collective-permute-start.16 = (bf16[3,72,384]{2,1,0:T(8,128)(2,1)S(1)}, bf16[3,72,384]{2,1,0:T(8,128)(2,1)S(1)}, u32[]{:S(2)}, u32[]{:S(2)}) collective-permute-start(bf16[3,72,384]{2,1,0:T(8,128)(2,1)S(1)} %get-tuple-element.128.refs_5_), channel_id=1, source_target_pairs={{0,2},{1,3},{2,0},{3,1},{4,6},{5,7},{6,4},{7,5},{8,10},{9,11},{10,... | collective-permute-start | bytes 497672 | tf_op jit(solution)/shard_map/ppermute | solution.py:933
  166.7 2.7 %collective-permute-done.8.refs_3_ = bf16[4,1,48,640]{3,2,1,0:T(8,128)(2,1)S(1)} collective-permute-done((bf16[4,1,48,640]{3,2,1,0:T(8,128)(2,1)S(1)}, bf16[4,1,48,640]{3,2,1,0:T(8,128)(2,1)S(1)}, u32[]{:S(2)}, u32[]{:S(2)}) %collective-permute-start.8) | collective-permute-done | bytes 245792 | tf_op jit(solution)/shard_map/ppermute | solution.py:933
  170.0 3.4 %collective-permute-done.16.refs_2_ = bf16[3,72,384]{2,1,0:T(8,128)(2,1)S(1)} collective-permute-done((bf16[3,72,384]{2,1,0:T(8,128)(2,1)S(1)}, bf16[3,72,384]{2,1,0:T(8,128)(2,1)S(1)}, u32[]{:S(2)}, u32[]{:S(2)}) %collective-permute-start.16) | collective-permute-done | bytes 165920 | tf_op jit(solution)/shard_map/ppermute | solution.py:933
  174.1 3.8 %collective-permute-start.13 = (bf16[1,48,640]{2,1,0:T(8,128)(2,1)S(1)}, bf16[1,48,640]{2,1,0:T(8,128)(2,1)S(1)}, u32[]{:S(2)}, u32[]{:S(2)}) collective-permute-start(bf16[1,48,640]{2,1,0:T(8,128)(2,1)S(1)} %get-tuple-element.130), channel_id=1, source_target_pairs={{0,1},{1,2},{2,3},{3,0},{4,5},{5,6},{6,7},{7,4},{8,9},{9,10},{10,1... | collective-permute-start | bytes 184328 | tf_op jit(solution)/shard_map/ppermute | solution.py:1145
  177.9 2.3 collective-permute-start.15
  180.2 3.4 %collective-permute-done.13.refs_2_ = bf16[1,48,640]{2,1,0:T(8,128)(2,1)S(1)} collective-permute-done((bf16[1,48,640]{2,1,0:T(8,128)(2,1)S(1)}, bf16[1,48,640]{2,1,0:T(8,128)(2,1)S(1)}, u32[]{:S(2)}, u32[]{:S(2)}) %collective-permute-start.13) | collective-permute-done | bytes 61472 | tf_op jit(solution)/shard_map/ppermute | solution.py:1145
  183.6 4.7 %collective-permute-done.14.refs_3_ = bf16[1,48,640]{2,1,0:T(8,128)(2,1)S(1)} collective-permute-done((bf16[1,48,640]{2,1,0:T(8,128)(2,1)S(1)}, bf16[1,48,640]{2,1,0:T(8,128)(2,1)S(1)}, u32[]{:S(2)}, u32[]{:S(2)}) %collective-permute-start.14) | collective-permute-done | bytes 61472 | tf_op jit(solution)/shard_map/ppermute | solution.py:1145
  194.0 6.4 %collective-permute-done.19.refs_4_ = bf16[1,48,640]{2,1,0:T(8,128)(2,1)S(1)} collective-permute-done((bf16[1,48,640]{2,1,0:T(8,128)(2,1)S(1)}, bf16[1,48,640]{2,1,0:T(8,128)(2,1)S(1)}, u32[]{:S(2)}, u32[]{:S(2)}) %collective-permute-start.19) | collective-permute-done | bytes 61472 | tf_op jit(solution)/shard_map/ppermute | solution.py:1145
  200.5 2.5 collective-permute-done.17.refs_2_
  204.2 3.5 %all-to-all-start.2 = ((bf16[4,576,256]{2,1,0:T(8,128)(2,1)}), bf16[4,576,256]{2,1,0:T(8,128)(2,1)S(1)}, u32[]{:S(2)}, u32[]{:S(2)}) async-start(bf16[4,576,256]{2,1,0:T(8,128)(2,1)} %get-tuple-element.141), calls=%async_computation.2 | async-start | bytes 2359296 | tf_op jit(solution)/shard_map/all_to_all | solution.py:1157
  213.2 5.4 %collective-permute-done.26.refs_4_ = bf16[2,3,72,384]{3,2,1,0:T(8,128)(2,1)S(1)} collective-permute-done((bf16[2,3,72,384]{3,2,1,0:T(8,128)(2,1)S(1)}, bf16[2,3,72,384]{3,2,1,0:T(8,128)(2,1)S(1)}, u32[]{:S(2)}, u32[]{:S(2)}) %collective-permute-start.26) | collective-permute-done | bytes 331808 | tf_op jit(solution)/shard_map/ppermute | solution.py:933
  218.6 6.5 %collective-permute-done.25.refs_2_ = bf16[2,3,72,384]{3,2,1,0:T(8,128)(2,1)S(1)} collective-permute-done((bf16[2,3,72,384]{3,2,1,0:T(8,128)(2,1)S(1)}, bf16[2,3,72,384]{3,2,1,0:T(8,128)(2,1)S(1)}, u32[]{:S(2)}, u32[]{:S(2)}) %collective-permute-start.25) | collective-permute-done | bytes 331808 | tf_op jit(solution)/shard_map/ppermute | solution.py:933
  225.9 2.5 join_line.1
  230.5 2.3 join_chips.1.refs_1_.refs_3_
  233.4 8.8 %collective-permute-done.31.refs_4_ = bf16[2,2,3,72,384]{4,3,2,1,0:T(8,128)(2,1)} collective-permute-done((bf16[2,2,3,72,384]{4,3,2,1,0:T(8,128)(2,1)}, bf16[2,2,3,72,384]{4,3,2,1,0:T(8,128)(2,1)}, u32[]{:S(2)}, u32[]{:S(2)}) %collective-permute-start.31) | collective-permute-done | bytes 663584 | tf_op jit(solution)/shard_map/ppermute | solution.py:933
  243.9 2.7 %join.2 = (f32[576,576]{1,0:T(8,128)}, f32[192,576]{1,0:T(8,128)}, f32[192,576]{1,0:T(8,128)}, f32[576,576]{1,0:T(8,128)}, f32[576,128]{1,0:T(8,128)S(1)}) custom-call(s32[4]{0:T(128)S(1)} %copy-done.18, bf16[4,4,1,48,640]{4,3,2,1,0:T(8,128)(2,1)S(1)} %copy-done.1, bf16[4,4,1,48,640]{4,3,2,1,0:T(8,128)(2,1)S(1)} %collective-permute-done.27.refs_2_, ...), custom_call_target="tpu_custom_call" | custom-call | flops 1000 | bytes 1000 | tf_op jit(solution)/shard_map/join/pallas_call | solution.py:376
  248.4 2.4 place.2.refs_2_
  252.9 2.4 place.3.refs_9_
  255.3 7.2 %join.3 = (f32[2,4,72,1536]{3,2,1,0:T(8,128)}, f32[2,4,72,1536]{3,2,1,0:T(8,128)}, f32[2,4,72,1536]{3,2,1,0:T(8,128)}) custom-call(s32[4]{0:T(128)} %copy-done.15, bf16[2,2,3,72,384]{4,3,2,1,0:T(8,128)(2,1)} %get-tuple-element.138.refs_5_.refs_1_, bf16[2,2,3,72,384]{4,3,2,1,0:T(8,128)(2,1)} %get-tuple-element.140.refs_2_, ...), custom_call_target="tpu_custom_call" | custom-call | flops 1000 | bytes 1000 | tf_op jit(solution)/shard_map/join/pallas_call | solution.py:376
  (164 shorter events, 57.0 us)
Async XLA Ops:
  0.7 43.9 %all-to-all-start = ((bf16[4,576,256]{2,1,0:T(8,128)(2,1)}), bf16[4,576,256]{2,1,0:T(8,128)(2,1)}, u32[]{:S(2)}, u32[]{:S(2)}) async-start(bf16[4,576,256]{2,1,0:T(8,128)(2,1)} %bitcast.39), calls=%async_computation | async-start | bytes 2359296 | tf_op jit(solution)/shard_map/all_to_all | solution.py:1157
  22.5 36.5 %collective-permute-start.1 = (bf16[576,256]{1,0:T(8,128)(2,1)S(1)}, bf16[576,256]{1,0:T(8,128)(2,1)S(1)}, u32[]{:S(2)}, u32[]{:S(2)}) collective-permute-start(bf16[576,256]{1,0:T(8,128)(2,1)S(1)} %get-tuple-element.88), channel_id=1, source_target_pairs={{0,2},{1,3},{2,0},{3,1},{4,6},{5,7},{6,4},{7,5},{8,10},{9,11},{10,... | collective-permute-start | bytes 884744 | tf_op jit(solution)/shard_map/ppermute | solution.py:1145
  25.4 33.5 %collective-permute-start.2 = (bf16[576,256]{1,0:T(8,128)(2,1)S(1)}, bf16[576,256]{1,0:T(8,128)(2,1)S(1)}, u32[]{:S(2)}, u32[]{:S(2)}) collective-permute-start(bf16[576,256]{1,0:T(8,128)(2,1)S(1)} %get-tuple-element.89), channel_id=1, source_target_pairs={{0,3},{1,0},{2,1},{3,2},{4,7},{5,4},{6,5},{7,6},{8,11},{9,8},{10,9... | collective-permute-start | bytes 884744 | tf_op jit(solution)/shard_map/ppermute | solution.py:1145
  26.9 32.0 %collective-permute-start = (bf16[576,256]{1,0:T(8,128)(2,1)S(1)}, bf16[576,256]{1,0:T(8,128)(2,1)S(1)}, u32[]{:S(2)}, u32[]{:S(2)}) collective-permute-start(bf16[576,256]{1,0:T(8,128)(2,1)S(1)} %get-tuple-element.86.refs_6_), channel_id=1, source_target_pairs={{0,1},{1,2},{2,3},{3,0},{4,5},{5,6},{6,7},{7,4},{8,9},{9,10},{10,1... | collective-permute-start | bytes 884744 | tf_op jit(solution)/shard_map/ppermute | solution.py:1145
  96.3 51.0 %all-to-all-start.1 = ((bf16[4,576,256]{2,1,0:T(8,128)(2,1)}), bf16[4,576,256]{2,1,0:T(8,128)(2,1)S(1)}, u32[]{:S(2)}, u32[]{:S(2)}) async-start(bf16[4,576,256]{2,1,0:T(8,128)(2,1)} %get-tuple-element.97), calls=%async_computation.1 | async-start | bytes 2359296 | tf_op jit(solution)/shard_map/all_to_all | solution.py:1157
  109.0 26.9 %collective-permute-start.5 = (bf16[2,2,3,72,384]{4,3,2,1,0:T(8,128)(2,1)}, bf16[2,2,3,72,384]{4,3,2,1,0:T(8,128)(2,1)S(1)}, u32[]{:S(2)}, u32[]{:S(2)}) collective-permute-start(bf16[2,2,3,72,384]{4,3,2,1,0:T(8,128)(2,1)} %get-tuple-element.114), channel_id=1, source_target_pairs={{0,16},{4,20},{8,24},{12,28},{16,0},{20,4},{24,8},{28,12},{1,17},{... | collective-permute-start | bytes 1990664 | tf_op jit(solution)/shard_map/ppermute | solution.py:933
  110.5 25.4 %collective-permute-start.4 = (bf16[2,2,3,72,384]{4,3,2,1,0:T(8,128)(2,1)}, bf16[2,2,3,72,384]{4,3,2,1,0:T(8,128)(2,1)S(1)}, u32[]{:S(2)}, u32[]{:S(2)}) collective-permute-start(bf16[2,2,3,72,384]{4,3,2,1,0:T(8,128)(2,1)} %get-tuple-element.109.refs_17_), channel_id=1, source_target_pairs={{0,8},{4,12},{8,0},{12,4},{16,24},{20,28},{24,16},{28,20},{1,9},{5... | collective-permute-start | bytes 1990664 | tf_op jit(solution)/shard_map/ppermute | solution.py:933
  140.7 10.5 %collective-permute-start.11 = (bf16[2,3,72,384]{3,2,1,0:T(8,128)(2,1)}, bf16[2,3,72,384]{3,2,1,0:T(8,128)(2,1)}, u32[]{:S(2)}, u32[]{:S(2)}) collective-permute-start(bf16[2,3,72,384]{3,2,1,0:T(8,128)(2,1)} %get-tuple-element.125), channel_id=1, source_target_pairs={{0,8},{4,12},{8,0},{12,4},{16,24},{20,28},{24,16},{28,20},{1,9},{5... | collective-permute-start | bytes 995336 | tf_op jit(solution)/shard_map/ppermute | solution.py:933
  141.3 10.2 %collective-permute-start.10 = (bf16[2,3,72,384]{3,2,1,0:T(8,128)(2,1)}, bf16[2,3,72,384]{3,2,1,0:T(8,128)(2,1)}, u32[]{:S(2)}, u32[]{:S(2)}) collective-permute-start(bf16[2,3,72,384]{3,2,1,0:T(8,128)(2,1)} %get-tuple-element.118.refs_3_), channel_id=1, source_target_pairs={{0,16},{4,20},{8,24},{12,28},{16,0},{20,4},{24,8},{28,12},{1,17},{... | collective-permute-start | bytes 995336 | tf_op jit(solution)/shard_map/ppermute | solution.py:933
  156.0 10.7 %collective-permute-start.7 = (bf16[4,1,48,640]{3,2,1,0:T(8,128)(2,1)S(1)}, bf16[4,1,48,640]{3,2,1,0:T(8,128)(2,1)S(1)}, u32[]{:S(2)}, u32[]{:S(2)}) collective-permute-start(bf16[4,1,48,640]{3,2,1,0:T(8,128)(2,1)S(1)} %copy-done.24), channel_id=1, source_target_pairs={{0,8},{4,12},{8,0},{12,4},{16,24},{20,28},{24,16},{28,20},{1,9},{5... | collective-permute-start | bytes 737288 | tf_op jit(solution)/shard_map/ppermute | solution.py:933
  157.5 11.9 %collective-permute-start.8 = (bf16[4,1,48,640]{3,2,1,0:T(8,128)(2,1)S(1)}, bf16[4,1,48,640]{3,2,1,0:T(8,128)(2,1)S(1)}, u32[]{:S(2)}, u32[]{:S(2)}) collective-permute-start(bf16[4,1,48,640]{3,2,1,0:T(8,128)(2,1)S(1)} %copy-done.22), channel_id=1, source_target_pairs={{0,16},{4,20},{8,24},{12,28},{16,0},{20,4},{24,8},{28,12},{1,17},{... | collective-permute-start | bytes 737288 | tf_op jit(solution)/shard_map/ppermute | solution.py:933
  158.0 11.4 %collective-permute-start.9 = (bf16[4,1,48,640]{3,2,1,0:T(8,128)(2,1)S(1)}, bf16[4,1,48,640]{3,2,1,0:T(8,128)(2,1)S(1)}, u32[]{:S(2)}, u32[]{:S(2)}) collective-permute-start(bf16[4,1,48,640]{3,2,1,0:T(8,128)(2,1)S(1)} %copy-done.20), channel_id=1, source_target_pairs={{0,24},{4,28},{8,16},{12,20},{16,8},{20,12},{24,0},{28,4},{1,25},{... | collective-permute-start | bytes 737288 | tf_op jit(solution)/shard_map/ppermute | solution.py:933
  174.0 14.9 %collective-permute-start.20 = (bf16[3,72,384]{2,1,0:T(8,128)(2,1)S(1)}, bf16[3,72,384]{2,1,0:T(8,128)(2,1)S(1)}, u32[]{:S(2)}, u32[]{:S(2)}) collective-permute-start(bf16[3,72,384]{2,1,0:T(8,128)(2,1)S(1)} %total.1.refs_5_.refs_1_), channel_id=1, source_target_pairs={{0,2},{1,3},{2,0},{3,1},{4,6},{5,7},{6,4},{7,5},{8,10},{9,11},{10,... | collective-permute-start | bytes 497672 | tf_op jit(solution)/shard_map/ppermute | solution.py:933
  174.1 9.5 %collective-permute-start.13 = (bf16[1,48,640]{2,1,0:T(8,128)(2,1)S(1)}, bf16[1,48,640]{2,1,0:T(8,128)(2,1)S(1)}, u32[]{:S(2)}, u32[]{:S(2)}) collective-permute-start(bf16[1,48,640]{2,1,0:T(8,128)(2,1)S(1)} %get-tuple-element.130), channel_id=1, source_target_pairs={{0,1},{1,2},{2,3},{3,0},{4,5},{5,6},{6,7},{7,4},{8,9},{9,10},{10,1... | collective-permute-start | bytes 184328 | tf_op jit(solution)/shard_map/ppermute | solution.py:1145
  177.9 10.5 %collective-permute-start.14 = (bf16[1,48,640]{2,1,0:T(8,128)(2,1)S(1)}, bf16[1,48,640]{2,1,0:T(8,128)(2,1)S(1)}, u32[]{:S(2)}, u32[]{:S(2)}) collective-permute-start(bf16[1,48,640]{2,1,0:T(8,128)(2,1)S(1)} %get-tuple-element.131), channel_id=1, source_target_pairs={{0,2},{1,3},{2,0},{3,1},{4,6},{5,7},{6,4},{7,5},{8,10},{9,11},{10,... | collective-permute-start | bytes 184328 | tf_op jit(solution)/shard_map/ppermute | solution.py:1145
  177.9 10.4 %collective-permute-start.15 = (bf16[1,48,640]{2,1,0:T(8,128)(2,1)S(1)}, bf16[1,48,640]{2,1,0:T(8,128)(2,1)S(1)}, u32[]{:S(2)}, u32[]{:S(2)}) collective-permute-start(bf16[1,48,640]{2,1,0:T(8,128)(2,1)S(1)} %get-tuple-element.132), channel_id=1, source_target_pairs={{0,3},{1,0},{2,1},{3,2},{4,7},{5,4},{6,5},{7,6},{8,11},{9,8},{10,9... | collective-permute-start | bytes 184328 | tf_op jit(solution)/shard_map/ppermute | solution.py:1145
  189.5 14.1 %collective-permute-start.24 = (bf16[2,3,72,384]{3,2,1,0:T(8,128)(2,1)S(1)}, bf16[2,3,72,384]{3,2,1,0:T(8,128)(2,1)S(1)}, u32[]{:S(2)}, u32[]{:S(2)}) collective-permute-start(bf16[2,3,72,384]{3,2,1,0:T(8,128)(2,1)S(1)} %join_far.1.refs_5_.refs_1_), channel_id=1, source_target_pairs={{0,1},{1,0},{2,3},{3,2},{4,5},{5,4},{6,7},{7,6},{8,9},{9,8},{10,11... | collective-permute-start | bytes 995336 | tf_op jit(solution)/shard_map/ppermute | solution.py:933
  190.8 9.7 %collective-permute-start.19 = (bf16[1,48,640]{2,1,0:T(8,128)(2,1)S(1)}, bf16[1,48,640]{2,1,0:T(8,128)(2,1)S(1)}, u32[]{:S(2)}, u32[]{:S(2)}) collective-permute-start(bf16[1,48,640]{2,1,0:T(8,128)(2,1)S(1)} %add_seq.1.refs_3_.refs_1_), channel_id=1, source_target_pairs={{0,3},{1,0},{2,1},{3,2},{4,7},{5,4},{6,5},{7,6},{8,11},{9,8},{10,9... | collective-permute-start | bytes 184328 | tf_op jit(solution)/shard_map/ppermute | solution.py:1145
  193.1 9.9 %collective-permute-start.17 = (bf16[1,48,640]{2,1,0:T(8,128)(2,1)S(1)}, bf16[1,48,640]{2,1,0:T(8,128)(2,1)S(1)}, u32[]{:S(2)}, u32[]{:S(2)}) collective-permute-start(bf16[1,48,640]{2,1,0:T(8,128)(2,1)S(1)} %add_seq.1.refs_3_.refs_1_), channel_id=1, source_target_pairs={{0,1},{1,2},{2,3},{3,0},{4,5},{5,6},{6,7},{7,4},{8,9},{9,10},{10,1... | collective-permute-start | bytes 184328 | tf_op jit(solution)/shard_map/ppermute | solution.py:1145
  204.2 47.6 %all-to-all-start.2 = ((bf16[4,576,256]{2,1,0:T(8,128)(2,1)}), bf16[4,576,256]{2,1,0:T(8,128)(2,1)S(1)}, u32[]{:S(2)}, u32[]{:S(2)}) async-start(bf16[4,576,256]{2,1,0:T(8,128)(2,1)} %get-tuple-element.141), calls=%async_computation.2 | async-start | bytes 2359296 | tf_op jit(solution)/shard_map/all_to_all | solution.py:1157
  207.8 10.8 %collective-permute-start.26 = (bf16[2,3,72,384]{3,2,1,0:T(8,128)(2,1)S(1)}, bf16[2,3,72,384]{3,2,1,0:T(8,128)(2,1)S(1)}, u32[]{:S(2)}, u32[]{:S(2)}) collective-permute-start(bf16[2,3,72,384]{3,2,1,0:T(8,128)(2,1)S(1)} %get-tuple-element.135.refs_3_), channel_id=1, source_target_pairs={{0,8},{4,12},{8,0},{12,4},{16,24},{20,28},{24,16},{28,20},{1,9},{5... | collective-permute-start | bytes 995336 | tf_op jit(solution)/shard_map/ppermute | solution.py:933
  209.1 16.0 %collective-permute-start.25 = (bf16[2,3,72,384]{3,2,1,0:T(8,128)(2,1)S(1)}, bf16[2,3,72,384]{3,2,1,0:T(8,128)(2,1)S(1)}, u32[]{:S(2)}, u32[]{:S(2)}) collective-permute-start(bf16[2,3,72,384]{3,2,1,0:T(8,128)(2,1)S(1)} %get-tuple-element.137.refs_1_.refs_5_), channel_id=1, source_target_pairs={{0,16},{4,20},{8,24},{12,28},{16,0},{20,4},{24,8},{28,12},{1,17},{... | collective-permute-start | bytes 995336 | tf_op jit(solution)/shard_map/ppermute | solution.py:933
  209.7 19.7 %collective-permute-start.23 = (bf16[4,1,48,640]{3,2,1,0:T(8,128)(2,1)S(1)}, bf16[4,1,48,640]{3,2,1,0:T(8,128)(2,1)S(1)}, u32[]{:S(2)}, u32[]{:S(2)}) collective-permute-start(bf16[4,1,48,640]{3,2,1,0:T(8,128)(2,1)S(1)} %join_seq.1.refs_3_.refs_1_), channel_id=1, source_target_pairs={{0,24},{4,28},{8,16},{12,20},{16,8},{20,12},{24,0},{28,4},{1,25},{... | collective-permute-start | bytes 737288 | tf_op jit(solution)/shard_map/ppermute | solution.py:933
  211.4 19.2 %collective-permute-start.22 = (bf16[4,1,48,640]{3,2,1,0:T(8,128)(2,1)S(1)}, bf16[4,1,48,640]{3,2,1,0:T(8,128)(2,1)}, u32[]{:S(2)}, u32[]{:S(2)}) collective-permute-start(bf16[4,1,48,640]{3,2,1,0:T(8,128)(2,1)S(1)} %join_seq.1.refs_3_.refs_1_), channel_id=1, source_target_pairs={{0,16},{4,20},{8,24},{12,28},{16,0},{20,4},{24,8},{28,12},{1,17},{... | collective-permute-start | bytes 737288 | tf_op jit(solution)/shard_map/ppermute | solution.py:933
  211.9 18.7 %collective-permute-start.21 = (bf16[4,1,48,640]{3,2,1,0:T(8,128)(2,1)S(1)}, bf16[4,1,48,640]{3,2,1,0:T(8,128)(2,1)}, u32[]{:S(2)}, u32[]{:S(2)}) collective-permute-start(bf16[4,1,48,640]{3,2,1,0:T(8,128)(2,1)S(1)} %join_seq.1.refs_3_.refs_1_), channel_id=1, source_target_pairs={{0,8},{4,12},{8,0},{12,4},{16,24},{20,28},{24,16},{28,20},{1,9},{5... | collective-permute-start | bytes 737288 | tf_op jit(solution)/shard_map/ppermute | solution.py:933
  228.3 13.8 %collective-permute-start.31 = (bf16[2,2,3,72,384]{4,3,2,1,0:T(8,128)(2,1)}, bf16[2,2,3,72,384]{4,3,2,1,0:T(8,128)(2,1)}, u32[]{:S(2)}, u32[]{:S(2)}) collective-permute-start(bf16[2,2,3,72,384]{4,3,2,1,0:T(8,128)(2,1)} %get-tuple-element.140.refs_2_), channel_id=1, source_target_pairs={{0,16},{4,20},{8,24},{12,28},{16,0},{20,4},{24,8},{28,12},{1,17},{... | collective-permute-start | bytes 1990664 | tf_op jit(solution)/shard_map/ppermute | solution.py:933
  228.9 13.3 %collective-permute-start.30 = (bf16[2,2,3,72,384]{4,3,2,1,0:T(8,128)(2,1)}, bf16[2,2,3,72,384]{4,3,2,1,0:T(8,128)(2,1)}, u32[]{:S(2)}, u32[]{:S(2)}) collective-permute-start(bf16[2,2,3,72,384]{4,3,2,1,0:T(8,128)(2,1)} %get-tuple-element.138.refs_5_.refs_1_), channel_id=1, source_target_pairs={{0,8},{4,12},{8,0},{12,4},{16,24},{20,28},{24,16},{28,20},{1,9},{5... | collective-permute-start | bytes 1990664 | tf_op jit(solution)/shard_map/ppermute | solution.py:933
  232.9 9.8 %collective-permute-start.27 = (bf16[4,4,1,48,640]{4,3,2,1,0:T(8,128)(2,1)}, bf16[4,4,1,48,640]{4,3,2,1,0:T(8,128)(2,1)S(1)}, u32[]{:S(2)}, u32[]{:S(2)}) collective-permute-start(bf16[4,4,1,48,640]{4,3,2,1,0:T(8,128)(2,1)} %join_chips.1.refs_1_.refs_3_), channel_id=1, source_target_pairs={{0,4},{4,0},{8,12},{12,8},{16,20},{20,16},{24,28},{28,24},{1,5},{5... | collective-permute-start | bytes 2949128 | tf_op jit(solution)/shard_map/ppermute | solution.py:933
  232.9 14.5 %collective-permute-start.29 = (bf16[2,2,3,72,384]{4,3,2,1,0:T(8,128)(2,1)}, bf16[2,2,3,72,384]{4,3,2,1,0:T(8,128)(2,1)S(1)}, u32[]{:S(2)}, u32[]{:S(2)}) collective-permute-start(bf16[2,2,3,72,384]{4,3,2,1,0:T(8,128)(2,1)} %get-tuple-element.140.refs_2_), channel_id=1, source_target_pairs={{0,4},{4,0},{8,12},{12,8},{16,20},{20,16},{24,28},{28,24},{1,5},{5... | collective-permute-start | bytes 1990664 | tf_op jit(solution)/shard_map/ppermute | solution.py:933
  233.4 14.0 %collective-permute-start.28 = (bf16[2,2,3,72,384]{4,3,2,1,0:T(8,128)(2,1)S(1)}, bf16[2,2,3,72,384]{4,3,2,1,0:T(8,128)(2,1)S(1)}, u32[]{:S(2)}, u32[]{:S(2)}) collective-permute-start(bf16[2,2,3,72,384]{4,3,2,1,0:T(8,128)(2,1)S(1)} %copy-done.31), channel_id=1, source_target_pairs={{0,4},{4,0},{8,12},{12,8},{16,20},{20,16},{24,28},{28,24},{1,5},{5... | collective-permute-start | bytes 1990664 | tf_op jit(solution)/shard_map/ppermute | solution.py:933
  242.2 13.1 %collective-permute-start.33 = (bf16[2,2,3,72,384]{4,3,2,1,0:T(8,128)(2,1)}, bf16[2,2,3,72,384]{4,3,2,1,0:T(8,128)(2,1)}, u32[]{:S(2)}, u32[]{:S(2)}) collective-permute-start(bf16[2,2,3,72,384]{4,3,2,1,0:T(8,128)(2,1)} %collective-permute-done.31.refs_4_), channel_id=1, source_target_pairs={{0,4},{4,0},{8,12},{12,8},{16,20},{20,16},{24,28},{28,24},{1,5},{5... | collective-permute-start | bytes 1990664 | tf_op jit(solution)/shard_map/ppermute | solution.py:933
  242.2 13.1 %collective-permute-start.32 = (bf16[2,2,3,72,384]{4,3,2,1,0:T(8,128)(2,1)}, bf16[2,2,3,72,384]{4,3,2,1,0:T(8,128)(2,1)}, u32[]{:S(2)}, u32[]{:S(2)}) collective-permute-start(bf16[2,2,3,72,384]{4,3,2,1,0:T(8,128)(2,1)} %collective-permute-done.30.refs_3_), channel_id=1, source_target_pairs={{0,4},{4,0},{8,12},{12,8},{16,20},{20,16},{24,28},{28,24},{1,5},{5... | collective-permute-start | bytes 1990664 | tf_op jit(solution)/shard_map/ppermute | solution.py:933
  (48 other events, 252.7 us)

commit v2 on v1

--- a/solution.py
+++ b/solution.py
@@ -1265,11 +1265,12 @@
     )
     Order.also = tuple(near_came)
     mixed_out = place(info, mixed_out)
-    far_came = [swap(part, "dp", 1) for part in wide_sum.next]
+    parts, Order.last = lax.optimization_barrier((wide_sum.next, Order.last))
+    far_came = [swap(part, "dp", 1) for part in parts]
     Order.also = (tokens_out,)
     tokens_out = place(info, tokens_out)
     w_gate_sum, w_up_sum, w_down_sum = join_wide(
-        info, TWO_ROUTES, [*wide_sum.outs, *wide_sum.next, *near_came, *far_came]
+        info, TWO_ROUTES, [*wide_sum.outs, *parts, *near_came, *far_came]
     )
     return (
         jnp.swapaxes(mixed_out, 1, 2),

time: 264 us -> 261 us (0.989)
  waiting for transfers between devices: 67.9 us -> 63.1 us
    ppermute x25, waiting for transfers between devices: 37.6 us -> 32.9 us  [swap(): return lax.ppermute(values, axis, [(k, k ^ bits) for k in range(count)])]
    unnamed x89 -> x93, local copies, waits for them, and re-layouts: 20.2 us -> 22.5 us
where the time goes in v2:
time: 261 us; the launch traced here: 260 us
  Pallas kernels  109 us (42%)
  waiting for transfers between devices  63.1 us (24%)
  starting transfers between devices  53.4 us (20%)
  local copies, waits for them, and re-layouts  31.2 us (12%)
    pallas_call x21, Pallas kernels, run(): pl.pallas_call(body, grid=grid, in_specs=[SMEM] + (in_specs or [FULL] * t...  109 us
    ppermute x25, waiting for transfers between devices, swap(): return lax.ppermute(values, axis, [(k, k ^ bits) for k in range(count)])  32.9 us
    unnamed x93, local copies, waits for them, and re-layouts  22.5 us
    ppermute x25, starting transfers between devices, swap(): return lax.ppermute(values, axis, [(k, k ^ bits) for k in range(count)])  21 us
    all_to_all x3, starting transfers between devices, exchange(): return lax.all_to_all(values, 'seq', 0, 0)  18 us
    ppermute x9, waiting for transfers between devices, shift(): return lax.ppermute(values, 'seq', [(k, (k + step) % 4) for k in range(4)])  17.1 us
    ppermute x9, starting transfers between devices, shift(): return lax.ppermute(values, 'seq', [(k, (k + step) % 4) for k in range(4)])  14.4 us
    all_to_all x3, waiting for transfers between devices, exchange(): return lax.all_to_all(values, 'seq', 0, 0)  13.2 us
  transfers between devices with their start and end apart: 37, of which 15 were waited for; matrix products, arithmetic and copies ran while one was open for 7% of the time, Pallas kernels for 24%

profile of v2, /device:TPU:0, one launch (start us, length us, event | category | flops | bytes accessed | tf_op | source)
XLA Modules:
  0.0 260.1 jit_solution(17547015367823922191)
XLA Ops:
  0.7 6.5 %all-to-all-start = ((bf16[4,576,256]{2,1,0:T(8,128)(2,1)}), bf16[4,576,256]{2,1,0:T(8,128)(2,1)}, u32[]{:S(2)}, u32[]{:S(2)}) async-start(bf16[4,576,256]{2,1,0:T(8,128)(2,1)} %bitcast.39), calls=%async_computation | async-start | bytes 2359296 | tf_op jit(solution)/shard_map/all_to_all | solution.py:1157
  11.8 2.3 copy.32
  14.1 4.0 %copy.33 = bf16[576,1536]{0,1:T(8,128)(2,1)} copy(bf16[576,1536]{1,0:T(8,128)(2,1)} %refs_14_.1) | data formatting | bytes 3538944 | tf_op args[7]
  22.5 3.0 %collective-permute-start.1 = (bf16[576,256]{1,0:T(8,128)(2,1)S(1)}, bf16[576,256]{1,0:T(8,128)(2,1)S(1)}, u32[]{:S(2)}, u32[]{:S(2)}) collective-permute-start(bf16[576,256]{1,0:T(8,128)(2,1)S(1)} %get-tuple-element.91), channel_id=1, source_target_pairs={{0,2},{1,3},{2,0},{3,1},{4,6},{5,7},{6,4},{7,5},{8,10},{9,11},{10,... | collective-permute-start | bytes 884744 | tf_op jit(solution)/shard_map/ppermute | solution.py:1145
  27.5 3.9 %copy.34.refs_12_ = bf16[1536,576]{1,0:T(8,128)(2,1)} copy(bf16[1536,576]{0,1:T(8,128)(2,1)} %param.20) | data formatting | bytes 3538944 | tf_op jit(solution)/shard_map/optimization_barrier | solution.py:1199
  31.4 13.2 %all-to-all-done.refs_1_.refs_11_ = bf16[4,576,256]{2,1,0:T(8,128)(2,1)} async-done(((bf16[4,576,256]{2,1,0:T(8,128)(2,1)}), bf16[4,576,256]{2,1,0:T(8,128)(2,1)}, u32[]{:S(2)}, u32[]{:S(2)}) %all-to-all-start) | async-done | bytes 1179680 | tf_op jit(solution)/shard_map/all_to_all | solution.py:1157
  44.6 14.4 %attend.1 = (bf16[4,576,256]{2,1,0:T(8,128)(2,1)}, bf16[3,4,192,256]{3,2,1,0:T(8,128)(2,1)}, bf16[3,4,64,256]{3,2,1,0:T(8,128)(2,1)}, bf16[3,4,64,256]{3,2,1,0:T...) custom-call(s32[4]{0:T(128)} %copy-done.15, ...), custom_call_target="tpu_custom_call" | custom-call | flops 1000 | bytes 1000 | tf_op jit(solution)/shard_map/attend/pallas_call | solution.py:376
  59.9 35.7 %ffn.1 = (bf16[4,576,256]{2,1,0:T(8,128)(2,1)}, f32[4,576,256]{2,1,0:T(8,128)}, bf16[4,576,256]{2,1,0:T(8,128)(2,1)}, bf16[4,576,256]{2,1,0:T(8,128)(2,1)}, f32[...) custom-call(s32[4]{0:T(128)S(1)} %copy-done.16, ...), custom_call_target="tpu_custom_call" | custom-call | flops 1000 | bytes 1000 | tf_op jit(solution)/shard_map/ffn/pallas_call | solution.py:376
  96.3 8.0 %all-to-all-start.1 = ((bf16[4,576,256]{2,1,0:T(8,128)(2,1)}), bf16[4,576,256]{2,1,0:T(8,128)(2,1)S(1)}, u32[]{:S(2)}, u32[]{:S(2)}) async-start(bf16[4,576,256]{2,1,0:T(8,128)(2,1)} %get-tuple-element.100), calls=%async_computation.1 | async-start | bytes 2359296 | tf_op jit(solution)/shard_map/all_to_all | solution.py:1157
  104.4 4.6 %split_plane.1 = (bf16[2,2,3,72,384]{4,3,2,1,0:T(8,128)(2,1)}, f32[2,2,3,72,384]{4,3,2,1,0:T(8,128)}, bf16[2,2,3,72,384]{4,3,2,1,0:T(8,128)(2,1)}, f32[2,2,3,72,384]{4,3,2,1,0:T(8,128)}) custom-call(s32[4]{0:T(128)} %copy-done.15, bf16[4,4,3,72,384]{4,3,2,1,0:T(8,128)(2,1)} %get-tuple-element.110.refs_1_, ...), custom_call_target="tpu_custom_call" | custom-call | flops 1000 | bytes 1000 | tf_op jit(solution)/shard_map/split_plane/pallas_call | solution.py:376
  112.0 23.9 %back.1 = (bf16[4,576,256]{2,1,0:T(8,128)(2,1)}, bf16[4,4,1,48,640]{4,3,2,1,0:T(8,128)(2,1)}, bf16[4,4,1,48,640]{4,3,2,1,0:T(8,128)(2,1)}) custom-call(s32[4]{0:T(128)} %copy-done.15, bf16[3,4,192,256]{3,2,1,0:T(8,128)(2,1)} %get-tuple-element.101.refs_1_, bf16[3,4,64,256]{3,2,1,0:T(8,128)(2,1)} %get-tuple-element.102.refs_2_, ...), custom_call_target="tpu_custom_call" | custom-call | flops 1000 | bytes 1000 | tf_op jit(solution)/shard_map/back/pallas_call | solution.py:376
  137.0 3.7 %split_line.1 = (bf16[2,3,72,384]{3,2,1,0:T(8,128)(2,1)}, f32[2,3,72,384]{3,2,1,0:T(8,128)}, bf16[2,3,72,384]{3,2,1,0:T(8,128)(2,1)}, f32[2,3,72,384]{3,2,1,0:T(8,128)}) custom-call(s32[4]{0:T(128)} %copy-done.15, f32[2,2,3,72,384]{4,3,2,1,0:T(8,128)} %get-tuple-element.115.refs_1_, bf16[2,2,3,72,384]{4,3,2,1,0:T(8,128)(2,1)} %copy-done.34, ...), custom_call_target="tpu_custom_call" | custom-call | flops 1000 | bytes 1000 | tf_op jit(solution)/shard_map/split_line/pallas_call | solution.py:376
  147.3 3.9 %collective-permute-done.11.refs_4_ = bf16[2,3,72,384]{3,2,1,0:T(8,128)(2,1)} collective-permute-done((bf16[2,3,72,384]{3,2,1,0:T(8,128)(2,1)}, bf16[2,3,72,384]{3,2,1,0:T(8,128)(2,1)}, u32[]{:S(2)}, u32[]{:S(2)}) %collective-permute-start.11) | collective-permute-done | bytes 331808 | tf_op jit(solution)/shard_map/ppermute | solution.py:933
  159.4 3.9 %collective-permute-done.12.refs_2_ = bf16[2,3,72,384]{3,2,1,0:T(8,128)(2,1)S(1)} collective-permute-done((bf16[2,3,72,384]{3,2,1,0:T(8,128)(2,1)S(1)}, bf16[2,3,72,384]{3,2,1,0:T(8,128)(2,1)S(1)}, u32[]{:S(2)}, u32[]{:S(2)}) %collective-permute-start.12) | collective-permute-done | bytes 331808 | tf_op jit(solution)/shard_map/ppermute | solution.py:933
  163.9 2.7 %collective-permute-start.16 = (bf16[3,72,384]{2,1,0:T(8,128)(2,1)S(1)}, bf16[3,72,384]{2,1,0:T(8,128)(2,1)S(1)}, u32[]{:S(2)}, u32[]{:S(2)}) collective-permute-start(bf16[3,72,384]{2,1,0:T(8,128)(2,1)S(1)} %get-tuple-element.131.refs_5_), channel_id=1, source_target_pairs={{0,2},{1,3},{2,0},{3,1},{4,6},{5,7},{6,4},{7,5},{8,10},{9,11},{10,... | collective-permute-start | bytes 497672 | tf_op jit(solution)/shard_map/ppermute | solution.py:933
  166.7 2.7 %collective-permute-done.8.refs_3_ = bf16[4,1,48,640]{3,2,1,0:T(8,128)(2,1)S(1)} collective-permute-done((bf16[4,1,48,640]{3,2,1,0:T(8,128)(2,1)S(1)}, bf16[4,1,48,640]{3,2,1,0:T(8,128)(2,1)S(1)}, u32[]{:S(2)}, u32[]{:S(2)}) %collective-permute-start.8) | collective-permute-done | bytes 245792 | tf_op jit(solution)/shard_map/ppermute | solution.py:933
  170.0 3.4 %collective-permute-done.16.refs_2_ = bf16[3,72,384]{2,1,0:T(8,128)(2,1)S(1)} collective-permute-done((bf16[3,72,384]{2,1,0:T(8,128)(2,1)S(1)}, bf16[3,72,384]{2,1,0:T(8,128)(2,1)S(1)}, u32[]{:S(2)}, u32[]{:S(2)}) %collective-permute-start.16) | collective-permute-done | bytes 165920 | tf_op jit(solution)/shard_map/ppermute | solution.py:933
  174.1 3.8 %collective-permute-start.13 = (bf16[1,48,640]{2,1,0:T(8,128)(2,1)S(1)}, bf16[1,48,640]{2,1,0:T(8,128)(2,1)S(1)}, u32[]{:S(2)}, u32[]{:S(2)}) collective-permute-start(bf16[1,48,640]{2,1,0:T(8,128)(2,1)S(1)} %get-tuple-element.133), channel_id=1, source_target_pairs={{0,1},{1,2},{2,3},{3,0},{4,5},{5,6},{6,7},{7,4},{8,9},{9,10},{10,1... | collective-permute-start | bytes 184328 | tf_op jit(solution)/shard_map/ppermute | solution.py:1145
  177.9 2.3 collective-permute-start.15
  180.2 3.4 %collective-permute-done.13.refs_2_ = bf16[1,48,640]{2,1,0:T(8,128)(2,1)S(1)} collective-permute-done((bf16[1,48,640]{2,1,0:T(8,128)(2,1)S(1)}, bf16[1,48,640]{2,1,0:T(8,128)(2,1)S(1)}, u32[]{:S(2)}, u32[]{:S(2)}) %collective-permute-start.13) | collective-permute-done | bytes 61472 | tf_op jit(solution)/shard_map/ppermute | solution.py:1145
  183.6 4.7 %collective-permute-done.14.refs_3_ = bf16[1,48,640]{2,1,0:T(8,128)(2,1)S(1)} collective-permute-done((bf16[1,48,640]{2,1,0:T(8,128)(2,1)S(1)}, bf16[1,48,640]{2,1,0:T(8,128)(2,1)S(1)}, u32[]{:S(2)}, u32[]{:S(2)}) %collective-permute-start.14) | collective-permute-done | bytes 61472 | tf_op jit(solution)/shard_map/ppermute | solution.py:1145
  194.0 6.4 %collective-permute-done.19.refs_4_ = bf16[1,48,640]{2,1,0:T(8,128)(2,1)S(1)} collective-permute-done((bf16[1,48,640]{2,1,0:T(8,128)(2,1)S(1)}, bf16[1,48,640]{2,1,0:T(8,128)(2,1)S(1)}, u32[]{:S(2)}, u32[]{:S(2)}) %collective-permute-start.19) | collective-permute-done | bytes 61472 | tf_op jit(solution)/shard_map/ppermute | solution.py:1145
  200.4 2.6 collective-permute-done.17.refs_2_
  209.6 3.5 %all-to-all-start.2 = ((bf16[4,576,256]{2,1,0:T(8,128)(2,1)}), bf16[4,576,256]{2,1,0:T(8,128)(2,1)S(1)}, u32[]{:S(2)}, u32[]{:S(2)}) async-start(bf16[4,576,256]{2,1,0:T(8,128)(2,1)} %get-tuple-element.144), calls=%async_computation.2 | async-start | bytes 2359296 | tf_op jit(solution)/shard_map/all_to_all | solution.py:1157
  215.0 6.6 %collective-permute-done.25.refs_2_ = bf16[2,3,72,384]{3,2,1,0:T(8,128)(2,1)S(1)} collective-permute-done((bf16[2,3,72,384]{3,2,1,0:T(8,128)(2,1)S(1)}, bf16[2,3,72,384]{3,2,1,0:T(8,128)(2,1)S(1)}, u32[]{:S(2)}, u32[]{:S(2)}) %collective-permute-start.25) | collective-permute-done | bytes 331808 | tf_op jit(solution)/shard_map/ppermute | solution.py:933
  222.4 2.5 join_line.1
  225.5 2.3 join_chips.1.refs_1_.refs_3_
  231.9 2.7 %join.2 = (f32[576,576]{1,0:T(8,128)}, f32[192,576]{1,0:T(8,128)}, f32[192,576]{1,0:T(8,128)}, f32[576,576]{1,0:T(8,128)}, f32[576,128]{1,0:T(8,128)S(1)}) custom-call(s32[4]{0:T(128)S(1)} %copy-done.18, bf16[4,4,1,48,640]{4,3,2,1,0:T(8,128)(2,1)S(1)} %copy-done.1, bf16[4,4,1,48,640]{4,3,2,1,0:T(8,128)(2,1)S(1)} %collective-permute-done.27.refs_2_, ...), custom_call_target="tpu_custom_call" | custom-call | flops 1000 | bytes 1000 | tf_op jit(solution)/shard_map/join/pallas_call | solution.py:376
  236.4 2.4 place.2.refs_2_
  238.8 7.2 %collective-permute-done.31.refs_4_ = bf16[2,2,3,72,384]{4,3,2,1,0:T(8,128)(2,1)} collective-permute-done((bf16[2,2,3,72,384]{4,3,2,1,0:T(8,128)(2,1)}, bf16[2,2,3,72,384]{4,3,2,1,0:T(8,128)(2,1)}, u32[]{:S(2)}, u32[]{:S(2)}) %collective-permute-start.31) | collective-permute-done | bytes 663584 | tf_op jit(solution)/shard_map/ppermute | solution.py:933
  248.6 2.4 place.3.refs_9_
  252.7 7.2 %join.3 = (f32[2,4,72,1536]{3,2,1,0:T(8,128)}, f32[2,4,72,1536]{3,2,1,0:T(8,128)}, f32[2,4,72,1536]{3,2,1,0:T(8,128)}) custom-call(s32[4]{0:T(128)} %copy-done.15, bf16[2,2,3,72,384]{4,3,2,1,0:T(8,128)(2,1)} %get-tuple-element.141.refs_5_.refs_1_, bf16[2,2,3,72,384]{4,3,2,1,0:T(8,128)(2,1)} %get-tuple-element.143.refs_2_, ...), custom_call_target="tpu_custom_call" | custom-call | flops 1000 | bytes 1000 | tf_op jit(solution)/shard_map/join/pallas_call | solution.py:376
  (168 shorter events, 59.1 us)
Async XLA Ops:
  0.7 43.9 %all-to-all-start = ((bf16[4,576,256]{2,1,0:T(8,128)(2,1)}), bf16[4,576,256]{2,1,0:T(8,128)(2,1)}, u32[]{:S(2)}, u32[]{:S(2)}) async-start(bf16[4,576,256]{2,1,0:T(8,128)(2,1)} %bitcast.39), calls=%async_computation | async-start | bytes 2359296 | tf_op jit(solution)/shard_map/all_to_all | solution.py:1157
  22.5 36.4 %collective-permute-start.1 = (bf16[576,256]{1,0:T(8,128)(2,1)S(1)}, bf16[576,256]{1,0:T(8,128)(2,1)S(1)}, u32[]{:S(2)}, u32[]{:S(2)}) collective-permute-start(bf16[576,256]{1,0:T(8,128)(2,1)S(1)} %get-tuple-element.91), channel_id=1, source_target_pairs={{0,2},{1,3},{2,0},{3,1},{4,6},{5,7},{6,4},{7,5},{8,10},{9,11},{10,... | collective-permute-start | bytes 884744 | tf_op jit(solution)/shard_map/ppermute | solution.py:1145
  25.5 33.5 %collective-permute-start.2 = (bf16[576,256]{1,0:T(8,128)(2,1)S(1)}, bf16[576,256]{1,0:T(8,128)(2,1)S(1)}, u32[]{:S(2)}, u32[]{:S(2)}) collective-permute-start(bf16[576,256]{1,0:T(8,128)(2,1)S(1)} %get-tuple-element.92), channel_id=1, source_target_pairs={{0,3},{1,0},{2,1},{3,2},{4,7},{5,4},{6,5},{7,6},{8,11},{9,8},{10,9... | collective-permute-start | bytes 884744 | tf_op jit(solution)/shard_map/ppermute | solution.py:1145
  26.9 32.0 %collective-permute-start = (bf16[576,256]{1,0:T(8,128)(2,1)S(1)}, bf16[576,256]{1,0:T(8,128)(2,1)S(1)}, u32[]{:S(2)}, u32[]{:S(2)}) collective-permute-start(bf16[576,256]{1,0:T(8,128)(2,1)S(1)} %get-tuple-element.89.refs_6_), channel_id=1, source_target_pairs={{0,1},{1,2},{2,3},{3,0},{4,5},{5,6},{6,7},{7,4},{8,9},{9,10},{10,1... | collective-permute-start | bytes 884744 | tf_op jit(solution)/shard_map/ppermute | solution.py:1145
  96.3 8.0 %collective-permute-start.3 = (bf16[4,4,3,72,384]{4,3,2,1,0:T(8,128)(2,1)}, bf16[4,4,3,72,384]{4,3,2,1,0:T(8,128)(2,1)}, u32[]{:S(2)}, u32[]{:S(2)}) collective-permute-start(bf16[4,4,3,72,384]{4,3,2,1,0:T(8,128)(2,1)} %get-tuple-element.111), channel_id=1, source_target_pairs={{0,4},{4,0},{8,12},{12,8},{16,20},{20,16},{24,28},{28,24},{1,5},{5... | collective-permute-start | bytes 7962632 | tf_op jit(solution)/shard_map/ppermute | solution.py:933
  96.3 51.0 %all-to-all-start.1 = ((bf16[4,576,256]{2,1,0:T(8,128)(2,1)}), bf16[4,576,256]{2,1,0:T(8,128)(2,1)S(1)}, u32[]{:S(2)}, u32[]{:S(2)}) async-start(bf16[4,576,256]{2,1,0:T(8,128)(2,1)} %get-tuple-element.100), calls=%async_computation.1 | async-start | bytes 2359296 | tf_op jit(solution)/shard_map/all_to_all | solution.py:1157
  109.0 26.9 %collective-permute-start.5 = (bf16[2,2,3,72,384]{4,3,2,1,0:T(8,128)(2,1)}, bf16[2,2,3,72,384]{4,3,2,1,0:T(8,128)(2,1)S(1)}, u32[]{:S(2)}, u32[]{:S(2)}) collective-permute-start(bf16[2,2,3,72,384]{4,3,2,1,0:T(8,128)(2,1)} %get-tuple-element.117), channel_id=1, source_target_pairs={{0,16},{4,20},{8,24},{12,28},{16,0},{20,4},{24,8},{28,12},{1,17},{... | collective-permute-start | bytes 1990664 | tf_op jit(solution)/shard_map/ppermute | solution.py:933
  110.5 25.4 %collective-permute-start.4 = (bf16[2,2,3,72,384]{4,3,2,1,0:T(8,128)(2,1)}, bf16[2,2,3,72,384]{4,3,2,1,0:T(8,128)(2,1)S(1)}, u32[]{:S(2)}, u32[]{:S(2)}) collective-permute-start(bf16[2,2,3,72,384]{4,3,2,1,0:T(8,128)(2,1)} %get-tuple-element.112.refs_17_), channel_id=1, source_target_pairs={{0,8},{4,12},{8,0},{12,4},{16,24},{20,28},{24,16},{28,20},{1,9},{5... | collective-permute-start | bytes 1990664 | tf_op jit(solution)/shard_map/ppermute | solution.py:933
  140.7 10.5 %collective-permute-start.11 = (bf16[2,3,72,384]{3,2,1,0:T(8,128)(2,1)}, bf16[2,3,72,384]{3,2,1,0:T(8,128)(2,1)}, u32[]{:S(2)}, u32[]{:S(2)}) collective-permute-start(bf16[2,3,72,384]{3,2,1,0:T(8,128)(2,1)} %get-tuple-element.128), channel_id=1, source_target_pairs={{0,8},{4,12},{8,0},{12,4},{16,24},{20,28},{24,16},{28,20},{1,9},{5... | collective-permute-start | bytes 995336 | tf_op jit(solution)/shard_map/ppermute | solution.py:933
  141.3 10.2 %collective-permute-start.10 = (bf16[2,3,72,384]{3,2,1,0:T(8,128)(2,1)}, bf16[2,3,72,384]{3,2,1,0:T(8,128)(2,1)}, u32[]{:S(2)}, u32[]{:S(2)}) collective-permute-start(bf16[2,3,72,384]{3,2,1,0:T(8,128)(2,1)} %get-tuple-element.121.refs_3_), channel_id=1, source_target_pairs={{0,16},{4,20},{8,24},{12,28},{16,0},{20,4},{24,8},{28,12},{1,17},{... | collective-permute-start | bytes 995336 | tf_op jit(solution)/shard_map/ppermute | solution.py:933
  153.9 9.5 %collective-permute-start.12 = (bf16[2,3,72,384]{3,2,1,0:T(8,128)(2,1)S(1)}, bf16[2,3,72,384]{3,2,1,0:T(8,128)(2,1)S(1)}, u32[]{:S(2)}, u32[]{:S(2)}) collective-permute-start(bf16[2,3,72,384]{3,2,1,0:T(8,128)(2,1)S(1)} %get-tuple-element.130.refs_3_), channel_id=1, source_target_pairs={{0,1},{1,0},{2,3},{3,2},{4,5},{5,4},{6,7},{7,6},{8,9},{9,8},{10,11... | collective-permute-start | bytes 995336 | tf_op jit(solution)/shard_map/ppermute | solution.py:933
  155.9 10.7 %collective-permute-start.7 = (bf16[4,1,48,640]{3,2,1,0:T(8,128)(2,1)S(1)}, bf16[4,1,48,640]{3,2,1,0:T(8,128)(2,1)S(1)}, u32[]{:S(2)}, u32[]{:S(2)}) collective-permute-start(bf16[4,1,48,640]{3,2,1,0:T(8,128)(2,1)S(1)} %copy-done.24), channel_id=1, source_target_pairs={{0,8},{4,12},{8,0},{12,4},{16,24},{20,28},{24,16},{28,20},{1,9},{5... | collective-permute-start | bytes 737288 | tf_op jit(solution)/shard_map/ppermute | solution.py:933
  157.5 11.9 %collective-permute-start.8 = (bf16[4,1,48,640]{3,2,1,0:T(8,128)(2,1)S(1)}, bf16[4,1,48,640]{3,2,1,0:T(8,128)(2,1)S(1)}, u32[]{:S(2)}, u32[]{:S(2)}) collective-permute-start(bf16[4,1,48,640]{3,2,1,0:T(8,128)(2,1)S(1)} %copy-done.22), channel_id=1, source_target_pairs={{0,16},{4,20},{8,24},{12,28},{16,0},{20,4},{24,8},{28,12},{1,17},{... | collective-permute-start | bytes 737288 | tf_op jit(solution)/shard_map/ppermute | solution.py:933
  157.9 11.4 %collective-permute-start.9 = (bf16[4,1,48,640]{3,2,1,0:T(8,128)(2,1)S(1)}, bf16[4,1,48,640]{3,2,1,0:T(8,128)(2,1)S(1)}, u32[]{:S(2)}, u32[]{:S(2)}) collective-permute-start(bf16[4,1,48,640]{3,2,1,0:T(8,128)(2,1)S(1)} %copy-done.20), channel_id=1, source_target_pairs={{0,24},{4,28},{8,16},{12,20},{16,8},{20,12},{24,0},{28,4},{1,25},{... | collective-permute-start | bytes 737288 | tf_op jit(solution)/shard_map/ppermute | solution.py:933
  163.9 9.5 %collective-permute-start.16 = (bf16[3,72,384]{2,1,0:T(8,128)(2,1)S(1)}, bf16[3,72,384]{2,1,0:T(8,128)(2,1)S(1)}, u32[]{:S(2)}, u32[]{:S(2)}) collective-permute-start(bf16[3,72,384]{2,1,0:T(8,128)(2,1)S(1)} %get-tuple-element.131.refs_5_), channel_id=1, source_target_pairs={{0,2},{1,3},{2,0},{3,1},{4,6},{5,7},{6,4},{7,5},{8,10},{9,11},{10,... | collective-permute-start | bytes 497672 | tf_op jit(solution)/shard_map/ppermute | solution.py:933
  174.0 14.9 %collective-permute-start.20 = (bf16[3,72,384]{2,1,0:T(8,128)(2,1)S(1)}, bf16[3,72,384]{2,1,0:T(8,128)(2,1)S(1)}, u32[]{:S(2)}, u32[]{:S(2)}) collective-permute-start(bf16[3,72,384]{2,1,0:T(8,128)(2,1)S(1)} %total.1.refs_5_.refs_1_), channel_id=1, source_target_pairs={{0,2},{1,3},{2,0},{3,1},{4,6},{5,7},{6,4},{7,5},{8,10},{9,11},{10,... | collective-permute-start | bytes 497672 | tf_op jit(solution)/shard_map/ppermute | solution.py:933
  174.1 9.6 %collective-permute-start.13 = (bf16[1,48,640]{2,1,0:T(8,128)(2,1)S(1)}, bf16[1,48,640]{2,1,0:T(8,128)(2,1)S(1)}, u32[]{:S(2)}, u32[]{:S(2)}) collective-permute-start(bf16[1,48,640]{2,1,0:T(8,128)(2,1)S(1)} %get-tuple-element.133), channel_id=1, source_target_pairs={{0,1},{1,2},{2,3},{3,0},{4,5},{5,6},{6,7},{7,4},{8,9},{9,10},{10,1... | collective-permute-start | bytes 184328 | tf_op jit(solution)/shard_map/ppermute | solution.py:1145
  177.9 10.5 %collective-permute-start.14 = (bf16[1,48,640]{2,1,0:T(8,128)(2,1)S(1)}, bf16[1,48,640]{2,1,0:T(8,128)(2,1)S(1)}, u32[]{:S(2)}, u32[]{:S(2)}) collective-permute-start(bf16[1,48,640]{2,1,0:T(8,128)(2,1)S(1)} %get-tuple-element.134), channel_id=1, source_target_pairs={{0,2},{1,3},{2,0},{3,1},{4,6},{5,7},{6,4},{7,5},{8,10},{9,11},{10,... | collective-permute-start | bytes 184328 | tf_op jit(solution)/shard_map/ppermute | solution.py:1145
  177.9 10.4 %collective-permute-start.15 = (bf16[1,48,640]{2,1,0:T(8,128)(2,1)S(1)}, bf16[1,48,640]{2,1,0:T(8,128)(2,1)S(1)}, u32[]{:S(2)}, u32[]{:S(2)}) collective-permute-start(bf16[1,48,640]{2,1,0:T(8,128)(2,1)S(1)} %get-tuple-element.135), channel_id=1, source_target_pairs={{0,3},{1,0},{2,1},{3,2},{4,7},{5,4},{6,5},{7,6},{8,11},{9,8},{10,9... | collective-permute-start | bytes 184328 | tf_op jit(solution)/shard_map/ppermute | solution.py:1145
  189.5 14.0 %collective-permute-start.24 = (bf16[2,3,72,384]{3,2,1,0:T(8,128)(2,1)S(1)}, bf16[2,3,72,384]{3,2,1,0:T(8,128)(2,1)S(1)}, u32[]{:S(2)}, u32[]{:S(2)}) collective-permute-start(bf16[2,3,72,384]{3,2,1,0:T(8,128)(2,1)S(1)} %join_far.1.refs_5_.refs_1_), channel_id=1, source_target_pairs={{0,1},{1,0},{2,3},{3,2},{4,5},{5,4},{6,7},{7,6},{8,9},{9,8},{10,11... | collective-permute-start | bytes 995336 | tf_op jit(solution)/shard_map/ppermute | solution.py:933
  190.8 9.6 %collective-permute-start.19 = (bf16[1,48,640]{2,1,0:T(8,128)(2,1)S(1)}, bf16[1,48,640]{2,1,0:T(8,128)(2,1)S(1)}, u32[]{:S(2)}, u32[]{:S(2)}) collective-permute-start(bf16[1,48,640]{2,1,0:T(8,128)(2,1)S(1)} %add_seq.1.refs_3_.refs_1_), channel_id=1, source_target_pairs={{0,3},{1,0},{2,1},{3,2},{4,7},{5,4},{6,5},{7,6},{8,11},{9,8},{10,9... | collective-permute-start | bytes 184328 | tf_op jit(solution)/shard_map/ppermute | solution.py:1145
  191.5 8.9 %collective-permute-start.18 = (bf16[1,48,640]{2,1,0:T(8,128)(2,1)S(1)}, bf16[1,48,640]{2,1,0:T(8,128)(2,1)S(1)}, u32[]{:S(2)}, u32[]{:S(2)}) collective-permute-start(bf16[1,48,640]{2,1,0:T(8,128)(2,1)S(1)} %add_seq.1.refs_3_.refs_1_), channel_id=1, source_target_pairs={{0,2},{1,3},{2,0},{3,1},{4,6},{5,7},{6,4},{7,5},{8,10},{9,11},{10,... | collective-permute-start | bytes 184328 | tf_op jit(solution)/shard_map/ppermute | solution.py:1145
  193.1 9.9 %collective-permute-start.17 = (bf16[1,48,640]{2,1,0:T(8,128)(2,1)S(1)}, bf16[1,48,640]{2,1,0:T(8,128)(2,1)S(1)}, u32[]{:S(2)}, u32[]{:S(2)}) collective-permute-start(bf16[1,48,640]{2,1,0:T(8,128)(2,1)S(1)} %add_seq.1.refs_3_.refs_1_), channel_id=1, source_target_pairs={{0,1},{1,2},{2,3},{3,0},{4,5},{5,6},{6,7},{7,4},{8,9},{9,10},{10,1... | collective-permute-start | bytes 184328 | tf_op jit(solution)/shard_map/ppermute | solution.py:1145
  204.2 10.8 %collective-permute-start.26 = (bf16[2,3,72,384]{3,2,1,0:T(8,128)(2,1)S(1)}, bf16[2,3,72,384]{3,2,1,0:T(8,128)(2,1)S(1)}, u32[]{:S(2)}, u32[]{:S(2)}) collective-permute-start(bf16[2,3,72,384]{3,2,1,0:T(8,128)(2,1)S(1)} %get-tuple-element.138.refs_3_), channel_id=1, source_target_pairs={{0,8},{4,12},{8,0},{12,4},{16,24},{20,28},{24,16},{28,20},{1,9},{5... | collective-permute-start | bytes 995336 | tf_op jit(solution)/shard_map/ppermute | solution.py:933
  205.6 16.0 %collective-permute-start.25 = (bf16[2,3,72,384]{3,2,1,0:T(8,128)(2,1)S(1)}, bf16[2,3,72,384]{3,2,1,0:T(8,128)(2,1)S(1)}, u32[]{:S(2)}, u32[]{:S(2)}) collective-permute-start(bf16[2,3,72,384]{3,2,1,0:T(8,128)(2,1)S(1)} %get-tuple-element.140.refs_1_.refs_5_), channel_id=1, source_target_pairs={{0,16},{4,20},{8,24},{12,28},{16,0},{20,4},{24,8},{28,12},{1,17},{... | collective-permute-start | bytes 995336 | tf_op jit(solution)/shard_map/ppermute | solution.py:933
  206.1 18.8 %collective-permute-start.23 = (bf16[4,1,48,640]{3,2,1,0:T(8,128)(2,1)S(1)}, bf16[4,1,48,640]{3,2,1,0:T(8,128)(2,1)S(1)}, u32[]{:S(2)}, u32[]{:S(2)}) collective-permute-start(bf16[4,1,48,640]{3,2,1,0:T(8,128)(2,1)S(1)} %join_seq.1.refs_3_.refs_1_), channel_id=1, source_target_pairs={{0,24},{4,28},{8,16},{12,20},{16,8},{20,12},{24,0},{28,4},{1,25},{... | collective-permute-start | bytes 737288 | tf_op jit(solution)/shard_map/ppermute | solution.py:933
  207.8 17.1 %collective-permute-start.22 = (bf16[4,1,48,640]{3,2,1,0:T(8,128)(2,1)S(1)}, bf16[4,1,48,640]{3,2,1,0:T(8,128)(2,1)}, u32[]{:S(2)}, u32[]{:S(2)}) collective-permute-start(bf16[4,1,48,640]{3,2,1,0:T(8,128)(2,1)S(1)} %join_seq.1.refs_3_.refs_1_), channel_id=1, source_target_pairs={{0,16},{4,20},{8,24},{12,28},{16,0},{20,4},{24,8},{28,12},{1,17},{... | collective-permute-start | bytes 737288 | tf_op jit(solution)/shard_map/ppermute | solution.py:933
  208.3 16.6 %collective-permute-start.21 = (bf16[4,1,48,640]{3,2,1,0:T(8,128)(2,1)S(1)}, bf16[4,1,48,640]{3,2,1,0:T(8,128)(2,1)}, u32[]{:S(2)}, u32[]{:S(2)}) collective-permute-start(bf16[4,1,48,640]{3,2,1,0:T(8,128)(2,1)S(1)} %join_seq.1.refs_3_.refs_1_), channel_id=1, source_target_pairs={{0,8},{4,12},{8,0},{12,4},{16,24},{20,28},{24,16},{28,20},{1,9},{5... | collective-permute-start | bytes 737288 | tf_op jit(solution)/shard_map/ppermute | solution.py:933
  209.6 38.0 %all-to-all-start.2 = ((bf16[4,576,256]{2,1,0:T(8,128)(2,1)}), bf16[4,576,256]{2,1,0:T(8,128)(2,1)S(1)}, u32[]{:S(2)}, u32[]{:S(2)}) async-start(bf16[4,576,256]{2,1,0:T(8,128)(2,1)} %get-tuple-element.144), calls=%async_computation.2 | async-start | bytes 2359296 | tf_op jit(solution)/shard_map/all_to_all | solution.py:1157
  227.9 7.4 %collective-permute-start.29 = (bf16[2,2,3,72,384]{4,3,2,1,0:T(8,128)(2,1)}, bf16[2,2,3,72,384]{4,3,2,1,0:T(8,128)(2,1)S(1)}, u32[]{:S(2)}, u32[]{:S(2)}) collective-permute-start(bf16[2,2,3,72,384]{4,3,2,1,0:T(8,128)(2,1)} %get-tuple-element.143.refs_2_), channel_id=1, source_target_pairs={{0,4},{4,0},{8,12},{12,8},{16,20},{20,16},{24,28},{28,24},{1,5},{5... | collective-permute-start | bytes 1990664 | tf_op jit(solution)/shard_map/ppermute | solution.py:933
  228.4 17.6 %collective-permute-start.31 = (bf16[2,2,3,72,384]{4,3,2,1,0:T(8,128)(2,1)}, bf16[2,2,3,72,384]{4,3,2,1,0:T(8,128)(2,1)}, u32[]{:S(2)}, u32[]{:S(2)}) collective-permute-start(bf16[2,2,3,72,384]{4,3,2,1,0:T(8,128)(2,1)} %get-tuple-element.143.refs_2_), channel_id=1, source_target_pairs={{0,16},{4,20},{8,24},{12,28},{16,0},{20,4},{24,8},{28,12},{1,17},{... | collective-permute-start | bytes 1990664 | tf_op jit(solution)/shard_map/ppermute | solution.py:933
  228.8 17.2 %collective-permute-start.30 = (bf16[2,2,3,72,384]{4,3,2,1,0:T(8,128)(2,1)S(1)}, bf16[2,2,3,72,384]{4,3,2,1,0:T(8,128)(2,1)}, u32[]{:S(2)}, u32[]{:S(2)}) collective-permute-start(bf16[2,2,3,72,384]{4,3,2,1,0:T(8,128)(2,1)S(1)} %copy-done.31), channel_id=1, source_target_pairs={{0,8},{4,12},{8,0},{12,4},{16,24},{20,28},{24,16},{28,20},{1,9},{5... | collective-permute-start | bytes 1990664 | tf_op jit(solution)/shard_map/ppermute | solution.py:933
  (50 other events, 226.2 us)
